TPU v7x, 32 devices: a whole 2x2x4 slice. The times are simulated.
32 devices in a mesh: seg: 4 (over y, x), sub: 8 (over z, core).
Axes of the slice: x: 2, y: 2, z: 4, core: 2. Of those that a mesh axis runs over, the one named last changes fastest.
Arguments:
- diffusivity: float32 [256, 4096], P('seg', 'sub'), may hold values from 0.01 to 0.4
- background_flow: float32 [256, 4096], P('seg', 'sub'), may hold values from 0.5 to 2
- inlet_modes: float32 [512, 4096], P(None, 'sub'), may hold values from -0.25 to 0.25
- profile_step: float32 [512], P('sub'), may hold values from -6 to 6
- brick_owner: int32 [8192, 1], P(('seg', 'sub')), may hold values from 0 to 7; in each aligned block of 256 rows (0 to 255, 256 to 511, ...) at most 64 rows name the same one
- voxel_row: int32 [8192], P(('seg', 'sub')), may hold values from 0 to 15
- noise_weight: float32 [512, 128], P(('seg', 'sub')), may hold values from 0.1 to 10
- spread_matrix: float32 [128, 128], replicated, may hold values from -0.5 to 0.5
Outputs:
- forward_field: float32 [256, 4096], P('seg', 'sub')
- response: float32 [512, 128], P(('seg', 'sub'))
- product: float32 [512], P(('seg', 'sub'))
Inputs may be any that keep to these rules, and one draw needn't show every extreme that they name: `brick_owner`: among the 256 blocks of one device each brick index is named at most 64 times, and exactly 64 times on some device; blocks go to bricks of their own segment group.
All inputs are finite; a program needn't handle non-finite values.
Results may differ from a plain program's by a relative error of at most 0.00019.
Values sent between devices are 32-bit elements; how exact they have to be, the bound alone decides.
A program may use at most 128 MiB of HBM per device.

v0:
```python
import jax
import jax.numpy as jnp
from jax import lax
from jax.sharding import PartitionSpec as P

NV = 2
SC = 2


SIGMA = 0.001
HIGH = lax.Precision.HIGHEST


def with_halo(block, sides, width):
    for axis, dim in sides:
        count = lax.axis_size(axis)
        forward = [(i, i + 1) for i in range(count - 1)]
        backward = [(target, source) for source, target in forward]
        low = lax.ppermute(
            lax.slice_in_dim(block, block.shape[dim] - width, None, axis=dim), axis, forward
        )
        high = lax.ppermute(lax.slice_in_dim(block, 0, width, axis=dim), axis, backward)
        block = jnp.concatenate([low, block, high], axis=dim)
    return block


def carried_in(value, axis, join, neutral, backward):
    count, mine = (lax.axis_size(axis), lax.axis_index(axis))
    pieces = jax.tree.map(lambda part: lax.all_gather(part, axis), value)
    if backward:
        pieces = jax.tree.map(lambda part: part[::-1], pieces)
        mine = count - 1 - mine
    so_far = jax.tree.map(
        lambda part, zero: jnp.full_like(part, 0) + jnp.asarray(zero, part.dtype), value, neutral
    )

    def turn(position, so_far):
        longer = join(so_far, jax.tree.map(lambda part: part[position], pieces))
        return jax.tree.map(lambda new, old: jnp.where(position < mine, new, old), longer, so_far)

    return lax.fori_loop(0, count - 1, turn, so_far)


def borders(stacked):
    return with_halo(stacked, (("seg", 1), ("sub", 2)), 1)


def neighbours(field):
    padded = borders(field[None])[0]
    return (padded[:-2, 1:-1], padded[2:, 1:-1], padded[1:-1, :-2], padded[1:-1, 2:])


def compose(earlier, latter):
    return (earlier[0] * latter[0], latter[0] * earlier[1] + latter[1])


def recurrence(gains, driving, reverse):
    part_gain, part_drive = lax.associative_scan(compose, (gains, driving), reverse=reverse, axis=0)
    boundary_row = 0 if reverse else -1
    totals = (part_gain[boundary_row], part_drive[boundary_row])
    identity = (jnp.ones_like(totals[0]), jnp.zeros_like(totals[1]))
    before = carried_in(totals, "seg", compose, identity, reverse)
    return part_gain * before[1][None, :] + part_drive


def apply_operator(field, stencil):
    diagonal, upstream, downstream, leftward, rightward = stencil
    above, below, left_side, right_side = neighbours(field)
    return (
        diagonal * field
        - upstream * above
        - downstream * below
        - leftward * left_side
        - rightward * right_side
    )


def relax(field, source, stencil, forward):
    diagonal, upstream, downstream, leftward, rightward = stencil
    above, below, left_side, right_side = neighbours(field)
    lateral = leftward * left_side + rightward * right_side
    if forward:
        explicit = source + downstream * below + lateral
        return recurrence(upstream / diagonal, explicit / diagonal, False)
    explicit = source + upstream * above + lateral
    return recurrence(downstream / diagonal, explicit / diagonal, True)


def restrict(field):
    height, breadth = field.shape
    return field.reshape(height // 2, 2, breadth // 2, 2).sum(axis=(1, 3))


def aggregate(field):
    return restrict(field) * 0.25


def prolong(field):
    return jnp.repeat(jnp.repeat(field, 2, axis=0), 2, axis=1)


def local_stencils(diffusion, flow, reaction):
    finest = (4.0 * diffusion + flow + reaction, diffusion + flow, diffusion, diffusion, diffusion)
    padded = borders(jnp.stack([diffusion, diffusion + flow]))
    adjoint = (
        finest[0],
        padded[0, :-2, 1:-1],
        padded[1, 2:, 1:-1],
        padded[0, 1:-1, :-2],
        padded[0, 1:-1, 2:],
    )
    return (finest, adjoint)


def vcycle(field, source, finest, coarse, forward):
    field = relax(field, source, finest, forward)
    coarse_source = restrict(source - apply_operator(field, finest))
    correction = jnp.zeros_like(coarse_source)
    for sweep_index in range(SC):
        correction = relax(correction, coarse_source, coarse, forward)
    field = field + prolong(correction)
    return relax(field, source, finest, forward)


def solve(source, finest, coarse, forward):
    field = jnp.zeros_like(source)
    for cycle_index in range(NV):
        field = vcycle(field, source, finest, coarse, forward)
    return field


def on_device(
    diffusivity,
    background_flow,
    inlet_modes,
    profile_step,
    brick_owner,
    voxel_row,
    noise_weight,
    spread_matrix,
):
    finest, finest_adjoint = local_stencils(diffusivity, background_flow, SIGMA)
    coarse, coarse_adjoint = local_stencils(
        aggregate(diffusivity), 2.0 * aggregate(background_flow), 4.0 * SIGMA
    )
    modes_all = lax.all_gather(profile_step, "sub", axis=0, tiled=True)
    profile = jnp.dot(modes_all, inlet_modes, precision=HIGH)
    at_inlet = lax.axis_index("seg") == 0
    inflow = diffusivity[0] + background_flow[0]
    source = jnp.zeros_like(diffusivity).at[0].set(jnp.where(at_inlet, inflow * profile, 0.0))
    forward_field = solve(source, finest, coarse, True)
    row_length = spread_matrix.shape[0]
    voxel_rows = noise_weight.shape[0]
    blocks = forward_field.reshape(-1, row_length)
    device_count = lax.axis_size("sub")
    owners = brick_owner[:, 0]
    target = owners * voxel_rows + voxel_row
    partial_sums = (
        jnp.zeros((device_count * voxel_rows, row_length), jnp.float32).at[target].add(blocks)
    )
    voxels = lax.psum_scatter(partial_sums, "sub", scatter_dimension=0, tiled=True)
    response = jnp.dot(voxels, spread_matrix.T, precision=HIGH)
    weighted = jnp.dot(noise_weight * response, spread_matrix, precision=HIGH)
    gathered = lax.all_gather(weighted, "sub", axis=0, tiled=True)
    driving = gathered[target]
    driving = driving.reshape(forward_field.shape)
    adjoint_field = solve(driving, finest_adjoint, coarse_adjoint, False)
    inlet_flux = jnp.where(at_inlet, inflow * adjoint_field[0], 0.0)
    product = lax.psum_scatter(
        jnp.dot(inlet_modes, inlet_flux, precision=HIGH),
        ("seg", "sub"),
        scatter_dimension=0,
        tiled=True,
    )
    return (forward_field, response, product)


def solution(mesh):
    return jax.shard_map(
        on_device,
        mesh=mesh,
        in_specs=(
            P("seg", "sub"),
            P("seg", "sub"),
            P(None, "sub"),
            P("sub"),
            P(("seg", "sub"), None),
            P(("seg", "sub")),
            P(("seg", "sub"), None),
            P(),
        ),
        out_specs=(P("seg", "sub"), P(("seg", "sub"), None), P(("seg", "sub"))),
        check_vma=False,
    )
```

profile of v0, /device:TPU:0, one launch (start us, length us, event | category | flops | bytes accessed | tf_op | source)
XLA Modules:
  0.0 647.9 jit_solution(210838619315610637)
XLA Ops:
  7.2 5.0 collective-permute-start
  13.5 4.5 collective-permute-start.8
  23.2 10.5 %reshape.127 = f32[32,2,256,2]{3,2,1,0:T(8,128)} reshape(f32[64,512]{1,0:T(8,128)} %param.42) | data formatting | bytes 262144 | tf_op jit(solution)/shard_map/reshape | solution.py:91
  33.7 9.7 %reshape.128 = f32[32,2,256,2]{3,2,1,0:T(8,128)} reshape(f32[64,512]{1,0:T(8,128)S(1)} %copy-done.2) | data formatting | bytes 262144 | tf_op jit(solution)/shard_map/reshape | solution.py:91
  44.9 15.8 %all-reduce.221 = f32[512]{0:T(512)S(1)} all-reduce(f32[512]{0:T(512)S(1)} %dynamic-update-slice.7), channel_id=1, replica_groups=mesh['seg'=4,'sub'=8] {'sub'}, use_global_device_ids=true, to_apply=%add.221 | all-reduce | flops 512 | bytes 4096
  60.6 4.6 reduce_sum.54
  65.2 4.6 reduce_sum.55
  81.0 12.3 %all-gather.1 = f32[4,1,512]{2,1,0:T(1,128)S(1)} all-gather(f32[1,1,512]{2,1,0:T(1,128)S(1)} %add_bitcast_fusion.18), channel_id=1, replica_groups=mesh['seg'=4,'sub'=8] {'seg'}, dimensions={0}, use_global_device_ids=true | all-gather | bytes 10240 | tf_op jit(solution)/shard_map/all_gather | solution.py:29
  93.4 8.3 %all-gather = f32[4,1,512]{2,1,0:T(1,128)S(1)} all-gather(f32[1,1,512]{2,1,0:T(1,128)S(1)} %add_bitcast_fusion.19), channel_id=1, replica_groups=mesh['seg'=4,'sub'=8] {'seg'}, dimensions={0}, use_global_device_ids=true | all-gather | bytes 10240 | tf_op jit(solution)/shard_map/all_gather | solution.py:29
  112.5 4.1 collective-permute-done.7
  116.9 9.7 %reshape.129 = f32[32,2,256,2]{3,2,1,0:T(8,128)} reshape(f32[64,512]{1,0:T(8,128)S(1)} %pad_subtract_fusion.1) | data formatting | bytes 262144 | tf_op jit(solution)/shard_map/reshape | solution.py:91
  126.6 4.6 reduce_sum.56
  132.3 8.9 %all-gather.3 = f32[4,1,256]{2,1,0:T(1,128)S(1)} all-gather(f32[1,1,256]{2,1,0:T(1,128)S(1)} %add_bitcast_fusion.28), channel_id=1, replica_groups=mesh['seg'=4,'sub'=8] {'seg'}, dimensions={0}, use_global_device_ids=true | all-gather | bytes 5120 | tf_op jit(solution)/shard_map/all_gather | solution.py:29
  141.3 6.5 %all-gather.2 = f32[4,1,256]{2,1,0:T(1,128)S(1)} all-gather(f32[1,1,256]{2,1,0:T(1,128)S(1)} %add_bitcast_fusion.29), channel_id=1, replica_groups=mesh['seg'=4,'sub'=8] {'seg'}, dimensions={0}, use_global_device_ids=true | all-gather | bytes 5120 | tf_op jit(solution)/shard_map/all_gather | solution.py:29
  153.3 4.1 collective-permute-done.13
  160.1 4.6 collective-permute-done.15
  165.5 8.9 %all-gather.4 = f32[4,1,256]{2,1,0:T(1,128)S(1)} all-gather(f32[1,1,256]{2,1,0:T(1,128)S(1)} %add_bitcast_fusion.27), channel_id=1, replica_groups=mesh['seg'=4,'sub'=8] {'seg'}, dimensions={0}, use_global_device_ids=true | all-gather | bytes 5120 | tf_op jit(solution)/shard_map/all_gather | solution.py:29
  177.9 4.2 collective-permute-done.17
  184.8 4.4 collective-permute-done.19
  190.6 9.2 %all-gather.5 = f32[4,1,512]{2,1,0:T(1,128)S(1)} all-gather(f32[1,1,512]{2,1,0:T(1,128)S(1)} %add_bitcast_fusion.17), channel_id=1, replica_groups=mesh['seg'=4,'sub'=8] {'seg'}, dimensions={0}, use_global_device_ids=true | all-gather | bytes 10240 | tf_op jit(solution)/shard_map/all_gather | solution.py:29
  203.2 4.2 collective-permute-done.21
  210.2 4.5 collective-permute-done.23
  216.0 8.9 %all-gather.6 = f32[4,1,512]{2,1,0:T(1,128)S(1)} all-gather(f32[1,1,512]{2,1,0:T(1,128)S(1)} %add_bitcast_fusion.16), channel_id=1, replica_groups=mesh['seg'=4,'sub'=8] {'seg'}, dimensions={0}, use_global_device_ids=true | all-gather | bytes 10240 | tf_op jit(solution)/shard_map/all_gather | solution.py:29
  228.4 4.6 collective-permute-start.37
  233.0 4.3 collective-permute-start.45
  240.4 4.1 collective-permute-done.27
  244.9 9.7 %reshape.132 = f32[32,2,256,2]{3,2,1,0:T(8,128)} reshape(f32[64,512]{1,0:T(8,128)S(1)} %pad_subtract_fusion) | data formatting | bytes 262144 | tf_op jit(solution)/shard_map/reshape | solution.py:91
  254.6 4.6 reduce_sum.57
  259.8 7.7 %all-gather.7 = f32[4,1,256]{2,1,0:T(1,128)S(1)} all-gather(f32[1,1,256]{2,1,0:T(1,128)S(1)} %add_bitcast_fusion.26), channel_id=1, replica_groups=mesh['seg'=4,'sub'=8] {'seg'}, dimensions={0}, use_global_device_ids=true | all-gather | bytes 5120 | tf_op jit(solution)/shard_map/all_gather | solution.py:29
  271.9 4.1 collective-permute-done.29
  278.9 4.3 collective-permute-done.31
  284.0 8.9 %all-gather.8 = f32[4,1,256]{2,1,0:T(1,128)S(1)} all-gather(f32[1,1,256]{2,1,0:T(1,128)S(1)} %add_bitcast_fusion.25), channel_id=1, replica_groups=mesh['seg'=4,'sub'=8] {'seg'}, dimensions={0}, use_global_device_ids=true | all-gather | bytes 5120 | tf_op jit(solution)/shard_map/all_gather | solution.py:29
  296.5 4.1 collective-permute-done.33
  303.3 4.4 collective-permute-done.35
  309.1 9.2 %all-gather.9 = f32[4,1,512]{2,1,0:T(1,128)S(1)} all-gather(f32[1,1,512]{2,1,0:T(1,128)S(1)} %add_bitcast_fusion.15), channel_id=1, replica_groups=mesh['seg'=4,'sub'=8] {'seg'}, dimensions={0}, use_global_device_ids=true | all-gather | bytes 10240 | tf_op jit(solution)/shard_map/all_gather | solution.py:29
  325.1 24.9 %reduce-scatter.2.cloned.1.call-done = f32[16,128]{1,0:T(8,128)} async-done(((f32[128,128]{1,0:T(8,128)}), f32[16,128]{1,0:T(8,128)}) %reduce-scatter.2.cloned.1.call-update) | async-done | bytes 8208 | tf_op jit(solution)/shard_map/reduce_scatter | solution.py:161
  351.1 14.0 %all_gather.90 = f32[128,128]{1,0:T(8,128)S(1)} all-gather(f32[16,128]{1,0:T(8,128)S(1)} %fusion.118), channel_id=1, replica_groups=mesh['seg'=4,'sub'=8] {'sub'}, dimensions={0}, use_global_device_ids=true | all-gather | bytes 73728 | tf_op jit(solution)/shard_map/all_gather | solution.py:164
  368.1 8.0 %all-gather.11 = f32[4,1,512]{2,1,0:T(1,128)S(1)} all-gather(f32[1,1,512]{2,1,0:T(1,128)S(1)} %add_bitcast_fusion.13), channel_id=1, replica_groups=mesh['seg'=4,'sub'=8] {'seg'}, dimensions={0}, use_global_device_ids=true | all-gather | bytes 10240 | tf_op jit(solution)/shard_map/all_gather | solution.py:29
  376.3 8.0 %all-gather.10 = f32[4,1,512]{2,1,0:T(1,128)S(1)} all-gather(f32[1,1,512]{2,1,0:T(1,128)S(1)} %add_bitcast_fusion.14), channel_id=1, replica_groups=mesh['seg'=4,'sub'=8] {'seg'}, dimensions={0}, use_global_device_ids=true | all-gather | bytes 10240 | tf_op jit(solution)/shard_map/all_gather | solution.py:29
  397.7 9.7 %reshape.137 = f32[32,2,256,2]{3,2,1,0:T(8,128)} reshape(f32[64,512]{1,0:T(8,128)S(1)} %fusion.18) | data formatting | bytes 262144 | tf_op jit(solution)/shard_map/reshape | solution.py:91
  407.4 4.6 reduce_sum.58
  413.4 8.9 %all-gather.13 = f32[4,1,256]{2,1,0:T(1,128)S(1)} all-gather(f32[1,1,256]{2,1,0:T(1,128)S(1)} %add_bitcast_fusion.23), channel_id=1, replica_groups=mesh['seg'=4,'sub'=8] {'seg'}, dimensions={0}, use_global_device_ids=true | all-gather | bytes 5120 | tf_op jit(solution)/shard_map/all_gather | solution.py:29
  422.3 6.5 %all-gather.12 = f32[4,1,256]{2,1,0:T(1,128)S(1)} all-gather(f32[1,1,256]{2,1,0:T(1,128)S(1)} %add_bitcast_fusion.24), channel_id=1, replica_groups=mesh['seg'=4,'sub'=8] {'seg'}, dimensions={0}, use_global_device_ids=true | all-gather | bytes 5120 | tf_op jit(solution)/shard_map/all_gather | solution.py:29
  434.5 4.1 collective-permute-done.49
  441.4 5.1 collective-permute-done.51
  447.5 9.2 %all-gather.14 = f32[4,1,256]{2,1,0:T(1,128)S(1)} all-gather(f32[1,1,256]{2,1,0:T(1,128)S(1)} %add_bitcast_fusion.22), channel_id=1, replica_groups=mesh['seg'=4,'sub'=8] {'seg'}, dimensions={0}, use_global_device_ids=true | all-gather | bytes 5120 | tf_op jit(solution)/shard_map/all_gather | solution.py:29
  460.4 4.2 collective-permute-done.53
  467.3 4.4 collective-permute-done.55
  473.3 9.2 %all-gather.15 = f32[4,1,512]{2,1,0:T(1,128)S(1)} all-gather(f32[1,1,512]{2,1,0:T(1,128)S(1)} %add_bitcast_fusion.12), channel_id=1, replica_groups=mesh['seg'=4,'sub'=8] {'seg'}, dimensions={0}, use_global_device_ids=true | all-gather | bytes 10240 | tf_op jit(solution)/shard_map/all_gather | solution.py:29
  486.2 4.2 collective-permute-done.57
  493.2 4.5 collective-permute-done.59
  499.2 8.9 %all-gather.16 = f32[4,1,512]{2,1,0:T(1,128)S(1)} all-gather(f32[1,1,512]{2,1,0:T(1,128)S(1)} %add_bitcast_fusion.11), channel_id=1, replica_groups=mesh['seg'=4,'sub'=8] {'seg'}, dimensions={0}, use_global_device_ids=true | all-gather | bytes 10240 | tf_op jit(solution)/shard_map/all_gather | solution.py:29
  511.8 4.2 collective-permute-done.61
  518.8 4.5 collective-permute-done.63
  523.6 9.7 %reshape.140 = f32[32,2,256,2]{3,2,1,0:T(8,128)} reshape(f32[64,512]{1,0:T(8,128)S(1)} %fusion.5) | data formatting | bytes 262144 | tf_op jit(solution)/shard_map/reshape | solution.py:91
  533.3 4.6 reduce_sum.59
  538.8 8.9 %all-gather.17 = f32[4,1,256]{2,1,0:T(1,128)S(1)} all-gather(f32[1,1,256]{2,1,0:T(1,128)S(1)} %add_bitcast_fusion.21), channel_id=1, replica_groups=mesh['seg'=4,'sub'=8] {'seg'}, dimensions={0}, use_global_device_ids=true | all-gather | bytes 5120 | tf_op jit(solution)/shard_map/all_gather | solution.py:29
  551.0 4.1 collective-permute-done.65
  558.0 4.4 collective-permute-done.67
  563.4 9.2 %all-gather.18 = f32[4,1,256]{2,1,0:T(1,128)S(1)} all-gather(f32[1,1,256]{2,1,0:T(1,128)S(1)} %add_bitcast_fusion.20), channel_id=1, replica_groups=mesh['seg'=4,'sub'=8] {'seg'}, dimensions={0}, use_global_device_ids=true | all-gather | bytes 5120 | tf_op jit(solution)/shard_map/all_gather | solution.py:29
  576.3 4.2 collective-permute-done.69
  583.2 4.4 collective-permute-done.71
  589.2 9.2 %all-gather.19 = f32[4,1,512]{2,1,0:T(1,128)S(1)} all-gather(f32[1,1,512]{2,1,0:T(1,128)S(1)} %add_bitcast_fusion.10), channel_id=1, replica_groups=mesh['seg'=4,'sub'=8] {'seg'}, dimensions={0}, use_global_device_ids=true | all-gather | bytes 10240 | tf_op jit(solution)/shard_map/all_gather | solution.py:29
  599.8 40.2 %all-reduce.222 = f32[512]{0:T(512)S(1)} all-reduce(f32[512]{0:T(512)S(1)} %bitcast.392), channel_id=3, replica_groups=mesh['seg'=4,'sub'=8] {'seg','sub'}, use_global_device_ids=true, to_apply=%region_40.41.clone | all-reduce | flops 512 | bytes 4096
  (1360 shorter events, 149.4 us)
Async XLA Ops:
  7.2 342.8 %reduce-scatter.2.cloned.1.call-start = ((), (), s32[]{:S(2)}) async-start(), calls=%async_computation.1 | async-start | bytes 73728 | tf_op jit(solution)/shard_map/reduce_scatter | solution.py:161
  7.2 64.6 %collective-permute-start = (f32[1,1,512]{2,1,0:T(1,128)S(1)}, f32[1,1,512]{2,1,0:T(1,128)S(1)}, u32[]{:S(2)}, u32[]{:S(2)}) collective-permute-start(f32[1,1,512]{2,1,0:T(1,128)S(1)} %broadcast.528), channel_id=1, source_target_pairs={{0,8},{8,16},{16,24},{1,9},{9,17},{17,25},{2,10},{10,18},{18,26},{... | collective-permute-start | bytes 6152 | tf_op jit(solution)/shard_map/ppermute | solution.py:19
  12.2 59.6 %collective-permute-start.1 = (f32[1,1,512]{2,1,0:T(1,128)S(1)}, f32[1,1,512]{2,1,0:T(1,128)S(1)}, u32[]{:S(2)}, u32[]{:S(2)}) collective-permute-start(f32[1,1,512]{2,1,0:T(1,128)S(1)} %broadcast.528), channel_id=1, source_target_pairs={{8,0},{16,8},{24,16},{9,1},{17,9},{25,17},{10,2},{18,10},{26,18},{... | collective-permute-start | bytes 6152 | tf_op jit(solution)/shard_map/ppermute | solution.py:22
  13.5 56.9 %collective-permute-start.8 = (f32[1,1,256]{2,1,0:T(1,128)S(1)}, f32[1,1,256]{2,1,0:T(1,128)S(1)}, u32[]{:S(2)}, u32[]{:S(2)}) collective-permute-start(f32[1,1,256]{2,1,0:T(1,128)S(1)} %broadcast.532), channel_id=1, source_target_pairs={{0,8},{8,16},{16,24},{1,9},{9,17},{17,25},{2,10},{10,18},{18,26},{... | collective-permute-start | bytes 3080 | tf_op jit(solution)/shard_map/ppermute | solution.py:19
  18.1 53.7 %collective-permute-start.9 = (f32[1,1,256]{2,1,0:T(1,128)S(1)}, f32[1,1,256]{2,1,0:T(1,128)S(1)}, u32[]{:S(2)}, u32[]{:S(2)}) collective-permute-start(f32[1,1,256]{2,1,0:T(1,128)S(1)} %broadcast.532), channel_id=1, source_target_pairs={{8,0},{16,8},{24,16},{9,1},{17,9},{25,17},{10,2},{18,10},{26,18},{... | collective-permute-start | bytes 3080 | tf_op jit(solution)/shard_map/ppermute | solution.py:22
  21.1 58.0 %collective-permute-start.36 = (f32[2,1,512]{2,1,0:T(1,128)S(1)}, f32[2,1,512]{2,1,0:T(1,128)S(1)}, u32[]{:S(2)}, u32[]{:S(2)}) collective-permute-start(f32[2,1,512]{2,1,0:T(1,128)S(1)} %get-tuple-element.2039), channel_id=1, source_target_pairs={{8,0},{16,8},{24,16},{9,1},{17,9},{25,17},{10,2},{18,10},{26,18},{... | collective-permute-start | bytes 12296 | tf_op jit(solution)/shard_map/ppermute | solution.py:22
  70.5 42.0 %collective-permute-start.40 = (f32[2,1,256]{2,1,0:T(1,128)S(1)}, f32[2,1,256]{2,1,0:T(1,128)S(1)}, u32[]{:S(2)}, u32[]{:S(2)}) collective-permute-start(f32[2,1,256]{2,1,0:T(1,128)S(1)} %get-tuple-element.2088), channel_id=1, source_target_pairs={{8,0},{16,8},{24,16},{9,1},{17,9},{25,17},{10,2},{18,10},{26,18},{... | collective-permute-start | bytes 6152 | tf_op jit(solution)/shard_map/ppermute | solution.py:22
  71.9 5.7 collective-permute-start.2
  73.3 5.6 collective-permute-start.3
  74.6 30.9 %collective-permute-start.10 = (f32[1,34,1]{2,1,0:T(8,128)S(1)}, f32[1,34,1]{2,1,0:T(8,128)S(1)}, u32[]{:S(2)}, u32[]{:S(2)}) collective-permute-start(f32[1,34,1]{2,1,0:T(8,128)S(1)} %get-tuple-element.2107), channel_id=1, source_target_pairs={{0,1},{1,2},{2,3},{3,4},{4,5},{5,6},{6,7},{8,9},{9,10},{10,11},{11... | collective-permute-start | bytes 416 | tf_op jit(solution)/shard_map/ppermute | solution.py:19
  77.6 27.8 %collective-permute-start.11 = (f32[1,34,1]{2,1,0:T(8,128)S(1)}, f32[1,34,1]{2,1,0:T(8,128)S(1)}, u32[]{:S(2)}, u32[]{:S(2)}) collective-permute-start(f32[1,34,1]{2,1,0:T(8,128)S(1)} %get-tuple-element.2108), channel_id=1, source_target_pairs={{1,0},{2,1},{3,2},{4,3},{5,4},{6,5},{7,6},{9,8},{10,9},{11,10},{12... | collective-permute-start | bytes 416 | tf_op jit(solution)/shard_map/ppermute | solution.py:22
  101.9 3.6 collective-permute-start.4
  104.1 5.5 collective-permute-start.5
  109.7 2.8 collective-permute-start.6
  111.0 5.6 collective-permute-start.7
  148.0 5.3 collective-permute-start.12
  152.0 5.5 collective-permute-start.13
  158.8 5.9 collective-permute-start.15
  175.0 2.9 collective-permute-start.16
  176.6 5.5 collective-permute-start.17
  183.5 5.8 collective-permute-start.19
  200.0 3.2 collective-permute-start.20
  201.9 5.5 collective-permute-start.21
  207.5 2.7 collective-permute-start.22
  208.9 5.8 collective-permute-start.23
  225.2 12.1 %collective-permute-start.24 = (f32[1,1,512]{2,1,0:T(1,128)S(1)}, f32[1,1,512]{2,1,0:T(1,128)S(1)}, u32[]{:S(2)}, u32[]{:S(2)}) collective-permute-start(f32[1,1,512]{2,1,0:T(1,128)S(1)} %get-tuple-element.2074), channel_id=1, source_target_pairs={{0,8},{8,16},{16,24},{1,9},{9,17},{17,25},{2,10},{10,18},{18,26},{... | collective-permute-start | bytes 6152 | tf_op jit(solution)/shard_map/ppermute | solution.py:19
  227.1 10.2 %collective-permute-start.25 = (f32[1,1,512]{2,1,0:T(1,128)S(1)}, f32[1,1,512]{2,1,0:T(1,128)S(1)}, u32[]{:S(2)}, u32[]{:S(2)}) collective-permute-start(f32[1,1,512]{2,1,0:T(1,128)S(1)} %get-tuple-element.2075), channel_id=1, source_target_pairs={{8,0},{16,8},{24,16},{9,1},{17,9},{25,17},{10,2},{18,10},{26,18},{... | collective-permute-start | bytes 6152 | tf_op jit(solution)/shard_map/ppermute | solution.py:22
  228.4 92.4 %collective-permute-start.37 = (f32[2,1,512]{2,1,0:T(1,128)S(1)}, f32[2,1,512]{2,1,0:T(1,128)S(1)}, u32[]{:S(2)}, u32[]{:S(2)}) collective-permute-start(f32[2,1,512]{2,1,0:T(1,128)S(1)} %get-tuple-element.2038), channel_id=1, source_target_pairs={{0,8},{8,16},{16,24},{1,9},{9,17},{17,25},{2,10},{10,18},{18,26},{... | collective-permute-start | bytes 12296 | tf_op jit(solution)/shard_map/ppermute | solution.py:19
  233.0 87.7 %collective-permute-start.45 = (f32[2,1,256]{2,1,0:T(1,128)S(1)}, f32[2,1,256]{2,1,0:T(1,128)S(1)}, u32[]{:S(2)}, u32[]{:S(2)}) collective-permute-start(f32[2,1,256]{2,1,0:T(1,128)S(1)} %get-tuple-element.2087), channel_id=1, source_target_pairs={{0,8},{8,16},{16,24},{1,9},{9,17},{17,25},{2,10},{10,18},{18,26},{... | collective-permute-start | bytes 6152 | tf_op jit(solution)/shard_map/ppermute | solution.py:19
  237.3 3.0 collective-permute-start.26
  239.1 5.5 collective-permute-start.27
  267.7 4.1 collective-permute-start.28
  270.5 5.5 collective-permute-start.29
  276.1 2.8 collective-permute-start.30
  277.4 5.9 collective-permute-start.31
  293.5 3.0 collective-permute-start.32
  295.2 5.5 collective-permute-start.33
  302.0 5.8 collective-permute-start.35
  320.9 45.0 %collective-permute-start.38 = (f32[2,66,1]{2,1,0:T(8,128)S(1)}, f32[2,66,1]{2,1,0:T(8,128)S(1)}, u32[]{:S(2)}, u32[]{:S(2)}) collective-permute-start(f32[2,66,1]{2,1,0:T(8,128)S(1)} %get-tuple-element.2037), channel_id=1, source_target_pairs={{0,1},{1,2},{2,3},{3,4},{4,5},{5,6},{6,7},{8,9},{9,10},{10,11},{11... | collective-permute-start | bytes 1592 | tf_op jit(solution)/shard_map/ppermute | solution.py:19
  323.4 42.4 %collective-permute-start.39 = (f32[2,66,1]{2,1,0:T(8,128)S(1)}, f32[2,66,1]{2,1,0:T(8,128)S(1)}, u32[]{:S(2)}, u32[]{:S(2)}) collective-permute-start(f32[2,66,1]{2,1,0:T(8,128)S(1)} %get-tuple-element.2036), channel_id=1, source_target_pairs={{1,0},{2,1},{3,2},{4,3},{5,4},{6,5},{7,6},{9,8},{10,9},{11,10},{12... | collective-permute-start | bytes 1592 | tf_op jit(solution)/shard_map/ppermute | solution.py:22
  384.9 5.2 collective-permute-start.41
  387.4 5.5 collective-permute-start.42
  388.8 23.1 %collective-permute-start.46 = (f32[2,34,1]{2,1,0:T(8,128)S(1)}, f32[2,34,1]{2,1,0:T(8,128)S(1)}, u32[]{:S(2)}, u32[]{:S(2)}) collective-permute-start(f32[2,34,1]{2,1,0:T(8,128)S(1)} %get-tuple-element.2086), channel_id=1, source_target_pairs={{0,1},{1,2},{2,3},{3,4},{4,5},{5,6},{6,7},{8,9},{9,10},{10,11},{11... | collective-permute-start | bytes 824 | tf_op jit(solution)/shard_map/ppermute | solution.py:19
  392.9 4.1 collective-permute-start.43
  394.2 3.1 collective-permute-start.44
  395.5 16.4 %collective-permute-start.47 = (f32[2,34,1]{2,1,0:T(8,128)S(1)}, f32[2,34,1]{2,1,0:T(8,128)S(1)}, u32[]{:S(2)}, u32[]{:S(2)}) collective-permute-start(f32[2,34,1]{2,1,0:T(8,128)S(1)} %get-tuple-element.2085), channel_id=1, source_target_pairs={{1,0},{2,1},{3,2},{4,3},{5,4},{6,5},{7,6},{9,8},{10,9},{11,10},{12... | collective-permute-start | bytes 824 | tf_op jit(solution)/shard_map/ppermute | solution.py:22
  429.3 5.3 collective-permute-start.48
  433.2 5.5 collective-permute-start.49
  440.1 6.4 collective-permute-start.51
  457.5 2.9 collective-permute-start.52
  459.1 5.5 collective-permute-start.53
  465.9 5.8 collective-permute-start.55
  483.0 3.2 collective-permute-start.56
  484.9 5.5 collective-permute-start.57
  491.8 5.8 collective-permute-start.59
  508.6 3.2 collective-permute-start.60
  510.5 5.5 collective-permute-start.61
  517.5 5.8 collective-permute-start.63
  548.1 3.0 collective-permute-start.64
  549.7 5.5 collective-permute-start.65
  556.7 5.7 collective-permute-start.67
  573.4 3.0 collective-permute-start.68
  575.0 5.5 collective-permute-start.69
  581.9 5.8 collective-permute-start.71
  (20 other events, 636.1 us)
Sparse Core Ops, SparseCore 0:
  320.7 29.2 reduce-scatter.1
where the time goes:
time: 657 us; the launch traced here: 648 us
  blocking collectives  245 us (37%)
  waiting for transfers between devices  136 us (21%)
  starting transfers between devices  123 us (19%)
  local copies, waits for them, and re-layouts  76 us (12%)
  other arithmetic  42.5 us (6%)
  between operations  21.7 us (3%)
    all_gather x20, blocking collectives, carried_in(): pieces = jax.tree.map(lambda part: lax.all_gather(part, axis), value)  175 us
    ppermute x36, waiting for transfers between devices, with_halo(): lax.ppermute(lax.slice_in_dim(block, 0, width, axis=dim), axis, backward)  111 us
    ppermute x36, starting transfers between devices, with_halo(): lax.ppermute(lax.slice_in_dim(block, block.shape[dim] - width, None, axis...  76.5 us
    reshape x6, local copies, waits for them, and re-layouts, restrict(): return field.reshape(height // 2, 2, breadth // 2, 2).sum(axis=(1, 3))  59 us
    unnamed x2, blocking collectives  56 us
    ppermute x36, starting transfers between devices, with_halo(): lax.ppermute(lax.slice_in_dim(block, 0, width, axis=dim), axis, backward)  46.9 us
    reduce_sum x6, other arithmetic, restrict(): return field.reshape(height // 2, 2, breadth // 2, 2).sum(axis=(1, 3))  27.4 us
    reduce_scatter x1, waiting for transfers between devices, on_device(): lax.psum_scatter(partial_sums, 'sub', scatter_dimension=0, tiled=True)  24.9 us
  transfers between devices with their start and end apart: 73, of which 28 were waited for; matrix products, arithmetic and copies ran while one was open for 11% of the time, Pallas kernels for 0%

commit v1 on v0

v1 whole, which is shorter than its diff:
```python
import functools

import jax
import jax.numpy as jnp
from jax import lax
from jax.experimental import pallas as pl
from jax.experimental.pallas import tpu as pltpu
from jax.sharding import PartitionSpec as P

NV = 2
SC = 2
SIGMA = 0.001
HIGH = lax.Precision.HIGHEST
MESH = pl.DeviceIdType.MESH
LANES = 128
HALF = LANES // 2
CHUNKS = 8
VMEM_BYTES = 48 * 1024 * 1024


def lane_shift(value, amount):
    width = value.shape[-1]
    return pltpu.roll(value, amount % width, axis=value.ndim - 1)


def chunk_shift(value, amount):
    return pltpu.roll(value, amount % value.shape[0], axis=0)


def chunk_index(shape):
    return lax.broadcasted_iota(jnp.int32, shape, 0)


def row_above(value):
    last = value[-1]
    moved = jnp.where(chunk_index(last.shape) > 0, chunk_shift(last, 1), 0.0)
    return jnp.concatenate([moved[None], value[:-1]], axis=0)


def row_below(value):
    first = value[0]
    keep = chunk_index(first.shape) < first.shape[0] - 1
    moved = jnp.where(keep, chunk_shift(first, -1), 0.0)
    return jnp.concatenate([value[1:], moved[None]], axis=0)


def add_columns(value):
    lane = lax.broadcasted_iota(jnp.int32, value.shape, value.ndim - 1)
    partner = jnp.where(lane % 2 == 0, lane_shift(value, -1), lane_shift(value, 1))
    return value + partner


def restrict(value):
    steps = value.shape[0]
    pairs = value.reshape((steps // 2, 2) + value.shape[1:])
    return add_columns(pairs[:, 0] + pairs[:, 1])


def make_plan(diffusion, flow, reaction, stride, forward, inside):
    inverse = 1.0 / (4.0 * diffusion + flow + reaction)
    if forward:
        ahead, gain = diffusion, (diffusion + flow) * inverse
        leftward, rightward = diffusion, diffusion
    else:
        ahead = row_above(diffusion)
        gain = row_below(diffusion + flow) * inverse
        leftward = lane_shift(diffusion, stride) * inside
        rightward = lane_shift(diffusion, -stride) * inside
    steps = gain.shape[0]
    order = range(steps) if forward else range(steps - 1, -1, -1)
    products, running = [None] * steps, None
    for step in order:
        running = gain[step] if running is None else running * gain[step]
        products[step] = running
    count = running.shape[0]
    chunk = chunk_index(running.shape)
    level, jumps, distance = running, [], 1
    while distance < count:
        if forward:
            keep, amount = chunk >= distance, distance
        else:
            keep, amount = chunk < count - distance, -distance
        level = jnp.where(keep, level, 0.0)
        jumps.append(level)
        level = level * chunk_shift(level, amount)
        distance *= 2
    return {
        "inverse": inverse,
        "ahead": ahead,
        "left": leftward,
        "right": rightward,
        "gain": gain,
        "products": jnp.stack(products),
        "jumps": jumps,
        "stride": stride,
        "forward": forward,
    }


def explicit_part(field, plan):
    stride = plan["stride"]
    beside = row_below(field) if plan["forward"] else row_above(field)
    return (
        plan["ahead"] * beside
        + plan["left"] * lane_shift(field, stride)
        + plan["right"] * lane_shift(field, -stride)
    )


def run_rows(driving, plan):
    forward, gain = plan["forward"], plan["gain"]
    steps, count = driving.shape[0], driving.shape[1]
    order = range(steps) if forward else range(steps - 1, -1, -1)
    local, running = [None] * steps, None
    for step in order:
        running = driving[step] if running is None else gain[step] * running + driving[step]
        local[step] = running
    total, distance = running, 1
    for jump in plan["jumps"]:
        total = total + jump * chunk_shift(total, distance if forward else -distance)
        distance *= 2
    chunk = chunk_index(total.shape)
    if forward:
        carry = jnp.where(chunk > 0, chunk_shift(total, 1), 0.0)
    else:
        carry = jnp.where(chunk < count - 1, chunk_shift(total, -1), 0.0)
    return jnp.stack(local) + plan["products"] * carry[None]


def solve(source, finest, coarse):
    field = None
    for cycle_index in range(NV):
        old = None if field is None else explicit_part(field, finest)
        total = source if old is None else source + old
        field = run_rows(total * finest["inverse"], finest)
        new = explicit_part(field, finest)
        coarse_source = restrict(new if old is None else new - old)
        correction = run_rows(coarse_source * coarse["inverse"], coarse)
        for sweep_index in range(1, SC):
            total = coarse_source + explicit_part(correction, coarse)
            correction = run_rows(total * coarse["inverse"], coarse)
        steps = field.shape[0]
        pairs = field.reshape((steps // 2, 2) + field.shape[1:]) + correction[:, None]
        field = pairs.reshape(field.shape)
        total = source + explicit_part(field, finest)
        field = run_rows(total * finest["inverse"], finest)
    return field


def plans(diffusion, flow, forward, inside):
    finest = make_plan(diffusion, flow, SIGMA, 1, forward, inside)
    coarse = make_plan(
        restrict(diffusion) * 0.25, restrict(flow) * 0.5, 4.0 * SIGMA, 2, forward, inside
    )
    return finest, coarse


def take_steps(ref, index):
    rows = ref.shape[-2]
    length = rows // CHUNKS
    halves = [
        jnp.stack([ref[index, half, pl.ds(step, CHUNKS, stride=length), :] for step in range(length)])
        for half in range(2)
    ]
    return jnp.concatenate(halves, axis=2)


def forward_kernel(strips_ref, profile_ref, field_ref):
    diffusion, flow = take_steps(strips_ref, 0), take_steps(strips_ref, 1)
    finest, coarse = plans(diffusion, flow, True, None)
    first = (diffusion[0] + flow[0]) * profile_ref[...]
    first = jnp.where(chunk_index(first.shape) == 0, first, 0.0)
    source = jnp.concatenate([first[None], jnp.zeros_like(diffusion[1:])], axis=0)
    field = solve(source, finest, coarse)
    length = field.shape[0]
    for step in range(length):
        field_ref[pl.ds(step, CHUNKS, stride=length), :] = field[step, :, :LANES]


def inside_mask(shape, strip, strips, group, groups):
    lane = lax.broadcasted_iota(jnp.int32, shape, len(shape) - 1)
    no_left = jnp.where((strip == 0) & (group == 0), 1, 0)
    no_right = jnp.where((strip == strips - 1) & (group == groups - 1), 1, 0)
    limit_high = jnp.where(no_left == 1, LANES + HALF, 2 * LANES)
    limit_low = jnp.where(no_right == 1, LANES, LANES + HALF)
    outside = (lane >= limit_high) | ((lane >= limit_low) & (lane < LANES + HALF))
    return jnp.where(outside, 0.0, 1.0)


def adjoint_kernel(seg, sub, strips_ref, driving_ref, modes_ref, partial_ref):
    strip, group = lax.axis_index("seg"), lax.axis_index("sub")
    diffusion, flow = take_steps(strips_ref, 0), take_steps(strips_ref, 1)
    inside = inside_mask((1, 1, 2 * LANES), strip, seg, group, sub)
    finest, coarse = plans(diffusion, flow, False, inside)
    field = solve(take_steps(driving_ref, 0), finest, coarse)
    flux = ((diffusion[0] + flow[0]) * field[0])[:, :LANES]
    flux = jnp.where(chunk_index(flux.shape) == 0, flux, 0.0)
    modes = modes_ref[:, pl.ds(pl.multiple_of(strip * LANES, LANES), LANES)]
    sums = lax.dot_general(
        flux, modes, (((1,), (1,)), ((), ())), precision=HIGH, preferred_element_type=jnp.float32
    )
    partial_ref[...] = sums


def enter(seg, sub, diagonal):
    strip, group = lax.axis_index("seg"), lax.axis_index("sub")
    barrier = pltpu.get_barrier_semaphore()

    def greet(to_strip, to_group):
        pl.semaphore_signal(barrier, inc=1, device_id=(to_strip, to_group), device_id_type=MESH)

    for k in range(1, seg):
        greet(lax.rem(strip + k, seg), group)
    for k in range(1, sub):
        greet(strip, lax.rem(group + k, sub))
    if diagonal:

        @pl.when(strip == 0)
        def _():
            for other in range(seg):
                greet(other, lax.rem(group + sub - 1, sub))

        @pl.when(strip == seg - 1)
        def _():
            for other in range(seg):
                greet(other, lax.rem(group + 1, sub))

    pl.semaphore_wait(barrier, seg - 1 + sub - 1 + (2 if diagonal else 0))


def remote(source, target, send, receive, to_strip, to_group):
    return pltpu.make_async_remote_copy(
        src_ref=source,
        dst_ref=target,
        send_sem=send,
        recv_sem=receive,
        device_id=(to_strip, to_group),
        device_id_type=MESH,
    )


def start_reshard(seg, sub, fields, packed, edges, strips_ref, edge_ref, sems):
    seg_send, seg_recv, edge_send, edge_recv = sems
    strip, group = lax.axis_index("seg"), lax.axis_index("sub")
    rows = packed.shape[3]
    lane = lax.broadcasted_iota(jnp.int32, (rows, LANES), 1)
    for index, field in enumerate(fields):
        edges[0, index] = field[:, (seg - 1) * LANES : seg * LANES]
        edges[1, index] = field[:, :LANES]
    here = pl.ds(pl.multiple_of(strip * rows, rows), rows)
    copies = [
        remote(edges.at[0], edge_ref.at[:, here, :], edge_send.at[0], edge_recv.at[strip],
               0, lax.rem(group + 1, sub)),
        remote(edges.at[1], edge_ref.at[:, here, :], edge_send.at[1], edge_recv.at[strip],
               seg - 1, lax.rem(group + sub - 1, sub)),
    ]
    for copy in copies:
        copy.start()
    for index, field in enumerate(fields):
        tiles = [field[:, t * LANES : (t + 1) * LANES] for t in range(seg)]
        for t in range(seg):
            packed[t, index, 0] = tiles[t]
            packed[t, index, 1] = jnp.where(
                lane < HALF, tiles[min(t + 1, seg - 1)], tiles[max(t - 1, 0)]
            )
    for k in range(1, seg):
        peer = lax.rem(strip + k, seg)
        copy = remote(packed.at[peer], strips_ref.at[:, :, here, :], seg_send.at[k], seg_recv.at[strip],
                      peer, group)
        copy.start()
        copies.append(copy)
    strips_ref[:, :, here, :] = packed[strip]
    return copies


def finish_reshard(seg, sub, copies, strips_ref, edge_ref, packed, sems):
    seg_send, seg_recv, edge_send, edge_recv = sems
    strip, group = lax.axis_index("seg"), lax.axis_index("sub")
    rows = packed.shape[3]
    for k in range(1, seg):
        peer = lax.rem(strip + k, seg)
        there = pl.ds(pl.multiple_of(peer * rows, rows), rows)
        remote(packed.at[peer], strips_ref.at[:, :, there, :], seg_send.at[k], seg_recv.at[peer],
               peer, group).wait_recv()

    def edge_arrivals():
        for other in range(seg):
            there = pl.ds(other * rows, rows)
            remote(packed.at[other, :, 0], edge_ref.at[:, there, :], edge_send.at[0],
                   edge_recv.at[other], 0, group).wait_recv()

    lane = lax.broadcasted_iota(jnp.int32, edge_ref.shape, 2)

    @pl.when(strip == 0)
    def _():
        edge_arrivals()
        known = jnp.where(group > 0, 1.0, 0.0)
        strips_ref[:, 1] = jnp.where(
            lane >= HALF, edge_ref[...] * known, strips_ref[:, 1]
        )

    @pl.when(strip == seg - 1)
    def _():
        edge_arrivals()
        known = jnp.where(group < sub - 1, 1.0, 0.0)
        strips_ref[:, 1] = jnp.where(
            lane < HALF, edge_ref[...] * known, strips_ref[:, 1]
        )

    for copy in copies:
        copy.wait_send()


def share(count, me, source_of, target_of, send, recv, place):
    started = []
    for k in range(1, count):
        peer = lax.rem(me + k, count)
        copy = remote(source_of(peer), target_of(me), send.at[k], recv.at[me], *place(peer))
        copy.start()
        started.append(copy)

    def arrive():
        for k in range(1, count):
            peer = lax.rem(me + count - k, count)
            remote(source_of(peer), target_of(peer), send.at[k], recv.at[peer],
                   *place(peer)).wait_recv()

    def left():
        for copy in started:
            copy.wait_send()

    return arrive, left


def intake_kernel(seg, sub, diffusivity_ref, flow_ref, modes_ref, step_ref, strips_ref, profile_ref,
                  packed, edges, edge_ref, steps, own, sides,
                  seg_send, seg_recv, edge_send, edge_recv, step_send, step_recv, side_send, side_recv):
    strip, group = lax.axis_index("seg"), lax.axis_index("sub")
    sems = (seg_send, seg_recv, edge_send, edge_recv)
    enter(seg, sub, True)
    arrive, left = share(
        sub, group, lambda peer: step_ref, lambda whose: steps.at[whose], step_send, step_recv,
        lambda peer: (strip, peer),
    )
    steps[group] = step_ref[...]
    copies = start_reshard(seg, sub, [diffusivity_ref[...], flow_ref[...]], packed, edges, strips_ref,
                           edge_ref, sems)
    arrive()
    depth = modes_ref.shape[0] // sub
    columns = steps[...].reshape(sub, LANES)
    total = None
    turned = columns.T
    for whose in range(sub):
        weight = turned[:depth, whose : whose + 1]
        term = weight * modes_ref[whose * depth : (whose + 1) * depth, :]
        total = term if total is None else total + term
    profile = jnp.sum(total, axis=0, keepdims=True)
    for t in range(seg):
        own[t + 1] = profile[:, t * LANES : (t + 1) * LANES]
    right = remote(own.at[seg], sides.at[0], side_send.at[0], side_recv.at[0],
                   strip, lax.rem(group + 1, sub))
    back = remote(own.at[1], sides.at[1], side_send.at[1], side_recv.at[1],
                  strip, lax.rem(group + sub - 1, sub))
    right.start()
    back.start()
    finish_reshard(seg, sub, copies, strips_ref, edge_ref, packed, sems)
    right.wait()
    back.wait()
    own[0] = sides[0]
    own[seg + 1] = sides[1]
    lane = lax.broadcasted_iota(jnp.int32, (1, LANES), 1)
    profile_ref[:, :LANES] = own[strip + 1]
    profile_ref[:, LANES:] = jnp.where(lane < HALF, own[strip + 2], own[strip])
    left()


def voxel_kernel(seg, sub, field_ref, target_row_ref, target_column_ref, noise_ref, spread_ref,
                 forward_ref, response_ref, driving_ref,
                 blocks, partial, arrived, weighted, gathered, packed, edges, edge_ref,
                 block_send, block_recv, sum_send, sum_recv, row_send, row_recv,
                 seg_send, seg_recv, edge_send, edge_recv):
    strip, group = lax.axis_index("seg"), lax.axis_index("sub")
    sems = (seg_send, seg_recv, edge_send, edge_recv)
    rows = blocks.shape[1]
    voxel_rows = noise_ref.shape[0]
    enter(seg, sub, True)

    def rows_of(whose):
        return pl.ds(pl.multiple_of(whose * rows, rows), rows)

    def voxels_of(whose):
        return pl.ds(pl.multiple_of(whose * voxel_rows, voxel_rows), voxel_rows)

    arrive, left_blocks = share(
        seg, strip, lambda peer: field_ref.at[rows_of(peer), :], lambda whose: blocks.at[whose],
        block_send, block_recv, lambda peer: (peer, group),
    )
    blocks[strip] = field_ref[rows_of(strip), :]
    arrive()
    total = None
    for t in range(seg):
        block = blocks[t]
        forward_ref[:, t * LANES : (t + 1) * LANES] = block
        voxel = lax.broadcasted_iota(jnp.int32, (sub * voxel_rows, rows), 0)
        chosen = jnp.where(voxel == target_row_ref[t : t + 1, :], 1.0, 0.0)
        term = jnp.dot(chosen, block, precision=HIGH, preferred_element_type=jnp.float32)
        total = term if total is None else total + term
    partial[...] = total
    arrive, left_sums = share(
        sub, group, lambda peer: partial.at[voxels_of(peer), :], lambda whose: arrived.at[whose],
        sum_send, sum_recv, lambda peer: (strip, peer),
    )
    arrived[group] = partial[voxels_of(group), :]
    arrive()
    voxels = arrived[0]
    for whose in range(1, sub):
        voxels = voxels + arrived[whose]
    spread = spread_ref[...]
    response = lax.dot_general(
        voxels, spread, (((1,), (1,)), ((), ())), precision=HIGH, preferred_element_type=jnp.float32
    )
    response_ref[...] = response
    weighted[...] = jnp.dot(
        noise_ref[...] * response, spread, precision=HIGH, preferred_element_type=jnp.float32
    )
    arrive, left_rows = share(
        sub, group, lambda peer: weighted, lambda whose: gathered.at[voxels_of(whose), :],
        row_send, row_recv, lambda peer: (strip, peer),
    )
    gathered[voxels_of(group), :] = weighted[...]
    arrive()
    everything = gathered[...]
    tiles = []
    for t in range(seg):
        voxel = lax.broadcasted_iota(jnp.int32, (rows, sub * voxel_rows), 1)
        chosen = jnp.where(voxel == target_column_ref[:, t : t + 1], 1.0, 0.0)
        tiles.append(jnp.dot(chosen, everything, precision=HIGH, preferred_element_type=jnp.float32))
    copies = start_reshard(seg, sub, [jnp.concatenate(tiles, axis=1)], packed, edges, driving_ref,
                           edge_ref, sems)
    finish_reshard(seg, sub, copies, driving_ref, edge_ref, packed, sems)
    left_blocks()
    left_sums()
    left_rows()


def product_kernel(seg, sub, partial_ref, product_ref, mine, arrived, second, total,
                   sub_send, sub_recv, seg_send, seg_recv):
    strip, group = lax.axis_index("seg"), lax.axis_index("sub")
    enter(seg, sub, False)
    mine[...] = partial_ref[0:1, :]
    arrive, left_first = share(
        sub, group, lambda peer: mine, lambda whose: arrived.at[whose], sub_send, sub_recv,
        lambda peer: (strip, peer),
    )
    arrived[group] = mine[...]
    arrive()
    value = arrived[0]
    for whose in range(1, sub):
        value = value + arrived[whose]
    total[...] = value
    arrive, left_second = share(
        seg, strip, lambda peer: total, lambda whose: second.at[whose], seg_send, seg_recv,
        lambda peer: (peer, group),
    )
    second[strip] = value
    arrive()
    value = second[0]
    for whose in range(1, seg):
        value = value + second[whose]
    product_ref[...] = value
    left_first()
    left_second()


def on_device(seg, sub, diffusivity, background_flow, inlet_modes, profile_step, brick_owner,
              voxel_row, noise_weight, spread_matrix):
    vmem = pl.BlockSpec(memory_space=pltpu.VMEM)
    f32 = jnp.float32
    rows, width = diffusivity.shape
    modes = inlet_modes.shape[0]
    voxel_rows = noise_weight.shape[0]
    total_rows = rows * seg
    dma = pltpu.SemaphoreType.DMA

    def call(kernel, shapes, scratch, collective):
        return pl.pallas_call(
            kernel,
            out_shape=[jax.ShapeDtypeStruct(shape, f32) for shape in shapes],
            out_specs=[vmem] * len(shapes),
            scratch_shapes=scratch,
            compiler_params=pltpu.CompilerParams(
                vmem_limit_bytes=VMEM_BYTES,
                **({} if collective is None else {"collective_id": collective, "has_side_effects": True}),
            ),
        )

    reshard_sems = [dma((seg,)), dma((seg,)), dma((2,)), dma((seg,))]
    step_row = jnp.pad(profile_step[None, :], ((0, 0), (0, LANES - profile_step.shape[0])))
    strips, profile = call(
        functools.partial(intake_kernel, seg, sub),
        [(2, 2, total_rows, LANES), (1, 2 * LANES)],
        [
            pltpu.VMEM((seg, 2, 2, rows, LANES), f32),
            pltpu.VMEM((2, 2, rows, LANES), f32),
            pltpu.VMEM((2, total_rows, LANES), f32),
            pltpu.VMEM((sub, 1, LANES), f32),
            pltpu.VMEM((seg + 2, 1, LANES), f32),
            pltpu.VMEM((2, 1, LANES), f32),
            *reshard_sems,
            dma((sub,)), dma((sub,)), dma((2,)), dma((2,)),
        ],
        0,
    )(diffusivity, background_flow, inlet_modes, step_row)
    (strip_field,) = call(forward_kernel, [(total_rows, LANES)], [], None)(strips, profile)
    target = (brick_owner[:, 0] * voxel_rows + voxel_row).reshape(rows, seg)
    forward_field, response, driving = call(
        functools.partial(voxel_kernel, seg, sub),
        [(rows, width), (voxel_rows, LANES), (1, 2, total_rows, LANES)],
        [
            pltpu.VMEM((seg, rows, LANES), f32),
            pltpu.VMEM((sub * voxel_rows, LANES), f32),
            pltpu.VMEM((sub, voxel_rows, LANES), f32),
            pltpu.VMEM((voxel_rows, LANES), f32),
            pltpu.VMEM((sub * voxel_rows, LANES), f32),
            pltpu.VMEM((seg, 1, 2, rows, LANES), f32),
            pltpu.VMEM((2, 1, rows, LANES), f32),
            pltpu.VMEM((1, total_rows, LANES), f32),
            dma((seg,)), dma((seg,)), dma((sub,)), dma((sub,)), dma((sub,)), dma((sub,)),
            *reshard_sems,
        ],
        1,
    )(strip_field, target.T, target, noise_weight, spread_matrix)
    (partial,) = call(functools.partial(adjoint_kernel, seg, sub), [(CHUNKS, modes)], [], None)(
        strips, driving, inlet_modes
    )
    (product,) = call(
        functools.partial(product_kernel, seg, sub),
        [(1, modes)],
        [
            pltpu.VMEM((1, modes), f32),
            pltpu.VMEM((sub, 1, modes), f32),
            pltpu.VMEM((seg, 1, modes), f32),
            pltpu.VMEM((1, modes), f32),
            dma((sub,)), dma((sub,)), dma((seg,)), dma((seg,)),
        ],
        2,
    )(partial)
    share_of = modes // (seg * sub)
    place = lax.axis_index("seg") * sub + lax.axis_index("sub")
    return (forward_field, response, lax.dynamic_slice(product[0], (place * share_of,), (share_of,)))


def solution(mesh):
    return jax.shard_map(
        functools.partial(on_device, mesh.shape["seg"], mesh.shape["sub"]),
        mesh=mesh,
        in_specs=(
            P("seg", "sub"),
            P("seg", "sub"),
            P(None, "sub"),
            P("sub"),
            P(("seg", "sub"), None),
            P(("seg", "sub")),
            P(("seg", "sub"), None),
            P(),
        ),
        out_specs=(P("seg", "sub"), P(("seg", "sub"), None), P(("seg", "sub"))),
        check_vma=False,
    )
```

time: 657 us -> 58 us (0.09); the launches traced: 648 us -> 57.8 us
  blocking collectives: 245 us -> 0 us
  waiting for transfers between devices: 136 us -> 0 us
  starting transfers between devices: 123 us -> 0 us
  local copies, waits for them, and re-layouts: 76 us -> 6.34 us
  Pallas kernels: 0 us -> 50.7 us
  other arithmetic: 42.5 us -> 0.01 us
  between operations: 21.7 us -> 0.76 us
    all_gather x21 -> x0, blocking collectives: 189 us -> none  [the longest x20 175 us: carried_in(): pieces = jax.tree.map(lambda part: lax.all_gather(part, axis), value)]
    ppermute x72 -> x0, starting transfers between devices: 123 us -> none  [the longest x36 76.5 us: with_halo(): lax.ppermute(lax.slice_in_dim(block, block.shape[dim] - width, None, axis...]
    ppermute x72 -> x0, waiting for transfers between devices: 111 us -> none  [the longest x36 111 us: with_halo(): lax.ppermute(lax.slice_in_dim(block, 0, width, axis=dim), axis, backward)]
    reshape x20 -> x2, local copies, waits for them, and re-layouts: 60 us -> 0.17 us  [on_device(): target = (brick_owner[:, 0] * voxel_rows + voxel_row).reshape(rows, seg)]
    unnamed x2 -> x0, blocking collectives: 56 us -> none
    pallas_call x0 -> x5, Pallas kernels: none -> 50.7 us  [the longest x1 20.7 us: on_device(): call(functools.partial(voxel_kernel, seg, sub), [(rows, width), (voxel_ro...]
    reduce_sum x6 -> x0, other arithmetic: 27.4 us -> none  [restrict(): return field.reshape(height // 2, 2, breadth // 2, 2).sum(axis=(1, 3))]
    reduce_scatter x1 -> x0, waiting for transfers between devices: 24.9 us -> none  [on_device(): lax.psum_scatter(partial_sums, 'sub', scatter_dimension=0, tiled=True)]
  transfers between devices with their start and end apart: 73 -> 0, of which waited for: 28 -> 0; matrix products, arithmetic and copies ran while one was open for 11% -> 0% of each run, Pallas kernels for 0% -> 0%
where the time goes in v1:
time: 58 us; the launch traced here: 57.8 us
  Pallas kernels  50.7 us (87%)
  local copies, waits for them, and re-layouts  6.34 us (11%)
  between operations  0.76 us (1%)
    pallas_call x1, Pallas kernels, on_device(): call(functools.partial(voxel_kernel, seg, sub), [(rows, width), (voxel_ro...  20.7 us
    pallas_call x1, Pallas kernels, on_device(): call(functools.partial(intake_kernel, seg, sub), [(2, 2, total_rows, LANE...  16.4 us
    pallas_call x1, Pallas kernels, on_device(): call(functools.partial(product_kernel, seg, sub), [(1, modes)], [pltpu.VM...  8.62 us
    unnamed x20, local copies, waits for them, and re-layouts  5.58 us
    pallas_call x1, Pallas kernels, on_device(): call(functools.partial(adjoint_kernel, seg, sub), [(CHUNKS, modes)], [],...  2.61 us
    pallas_call x1, Pallas kernels, on_device(): call(forward_kernel, [(total_rows, LANES)], [], None)(strips, profile)  2.28 us

profile of v1, /device:TPU:0, one launch (start us, length us, event | category | flops | bytes accessed | tf_op | source)
XLA Modules:
  0.0 57.8 jit_solution(17456214891349124730)
XLA Ops:
  0.6 0.0 copy-start.8
  0.6 0.6 %copy-done.8 = f32[64]{0:T(128)S(1)} copy-done((f32[64]{0:T(128)S(1)}, f32[64]{0:T(128)}, u32[]{:S(2)}) %copy-start.8) | copy-done | bytes 280
  1.3 0.0 copy-start
  1.3 1.2 %copy-done = f32[512,512]{1,0:T(8,128)S(1)} copy-done((f32[512,512]{1,0:T(8,128)S(1)}, f32[512,512]{1,0:T(8,128)}, u32[]{:S(2)}) %copy-start) | copy-done | bytes 1048600
  2.5 0.0 copy-start.2
  2.5 0.9 %copy-done.2 = f32[64,512]{1,0:T(8,128)S(1)} copy-done((f32[64,512]{1,0:T(8,128)S(1)}, f32[64,512]{1,0:T(8,128)}, u32[]{:S(2)}) %copy-start.2) | copy-done | bytes 131096
  3.4 0.0 copy-start.3
  3.4 0.9 %copy-done.3 = f32[64,512]{1,0:T(8,128)S(1)} copy-done((f32[64,512]{1,0:T(8,128)S(1)}, f32[64,512]{1,0:T(8,128)}, u32[]{:S(2)}) %copy-start.3) | copy-done | bytes 131096
  4.3 0.0 copy-start.1
  4.3 16.4 %shard_map.103 = (f32[2,2,256,128]{3,2,1,0:T(8,128)S(1)}, f32[1,256]{1,0:T(1,128)S(1)}) custom-call(f32[64,512]{1,0:T(8,128)S(1)} %copy-done.2, f32[64,512]{1,0:T(8,128)S(1)} %copy-done.3, f32[512,512]{1,0:T(8,128)S(1)} %copy-done, f32[1,128]{1,0:T(1,128)S(1)} %pad.4.step_ref), custom_call_target="tpu_custom_call" | custom-call | tf_op jit(solution)/shard_map/pallas_call | solution.py:499
  20.8 0.0 copy-start.7
  20.8 0.0 copy-start.6
  20.8 2.3 %shard_map.104.field_ref = f32[256,128]{1,0:T(8,128)S(1)} custom-call(f32[2,2,256,128]{3,2,1,0:T(8,128)S(1)} %get-tuple-element.8.strips_ref, f32[1,256]{1,0:T(1,128)S(1)} %get-tuple-element.9.profile_ref), custom_call_target="tpu_custom_call" | custom-call | tf_op jit(solution)/shard_map/pallas_call | solution.py:514
  23.1 0.0 copy-done.7
  23.1 0.0 copy-start.4
  23.1 0.0 copy-done.6
  23.1 0.1 reshape.12.target_column_ref
  23.2 0.0 copy-start.5
  23.3 0.1 copy.12
  23.3 0.6 %copy-done.4 = f32[128,128]{1,0:T(8,128)S(1)} copy-done((f32[128,128]{1,0:T(8,128)S(1)}, f32[128,128]{1,0:T(8,128)}, u32[]{:S(2)}) %copy-start.4) | copy-done | bytes 65560
  23.9 0.0 copy-done.5
  24.0 20.7 %shard_map.105 = (f32[64,512]{1,0:T(8,128)S(1)}, f32[16,128]{1,0:T(8,128)S(1)}, f32[1,2,256,128]{3,2,1,0:T(8,128)S(1)}) custom-call(f32[256,128]{1,0:T(8,128)S(1)} %shard_map.104.field_ref, s32[4,64]{1,0:T(4,128)S(1)} %bitcast.5, s32[64,4]{1,0:T(8,128)S(1)} %reshape.12.target_column_ref, f32[16,128]{1,0:T(8,128)S(1)} %copy-done.5, f32[128,128]{1,0:T(8,128)S(1)} %copy-done.4), custom_call_target="tpu_custom_call" | custom-call | tf_op jit(solution)/shard_map/pallas_call | solution.py:516
  44.7 0.0 copy-done.1
  44.7 2.6 %shard_map.106.partial_ref = f32[8,512]{1,0:T(8,128)S(1)} custom-call(f32[2,2,256,128]{3,2,1,0:T(8,128)S(1)} %get-tuple-element.8.strips_ref, f32[1,2,256,128]{3,2,1,0:T(8,128)S(1)} %get-tuple-element.12.driving_ref, f32[512,512]{1,0:T(8,128)S(1)} %copy-done.1), custom_call_target="tpu_custom_call" | custom-call | tf_op jit(solution)/shard_map/pallas_call | solution.py:533
  47.3 8.6 %shard_map.107 = f32[1,512]{1,0:T(1,128)S(1)} custom-call(f32[8,512]{1,0:T(8,128)S(1)} %shard_map.106.partial_ref), custom_call_target="tpu_custom_call" | custom-call | tf_op jit(solution)/shard_map/pallas_call | solution.py:536
  55.9 0.6 %dynamic-slice_bitcast_fusion = f32[16]{0:T(128)} fusion(f32[1,512]{1,0:T(1,128)S(1)} %shard_map.107, s32[]{:T(128)S(6)} %select_n.3), kind=kLoop, calls=%fused_computation | loop fusion | bytes 132 | tf_op jit(solution)/shard_map/dynamic_slice | solution.py:550
  56.5 0.7 %copy.15 = f32[64,512]{1,0:T(8,128)} copy(f32[64,512]{1,0:T(8,128)S(1)} %get-tuple-element.16) | data formatting | bytes 262144
  57.2 0.6 %copy.16 = f32[16,128]{1,0:T(8,128)} copy(f32[16,128]{1,0:T(8,128)S(1)} %get-tuple-element.17) | data formatting | bytes 16384
  (3 shorter events, 0.0 us)
Async XLA Ops:
  0.6 0.7 %copy-start.8 = (f32[64]{0:T(128)S(1)}, f32[64]{0:T(128)}, u32[]{:S(2)}) copy-start(f32[64]{0:T(128)} %param.11) | copy-start | bytes 772
  1.3 1.2 %copy-start = (f32[512,512]{1,0:T(8,128)S(1)}, f32[512,512]{1,0:T(8,128)}, u32[]{:S(2)}) copy-start(f32[512,512]{1,0:T(8,128)} %modes_ref.3) | copy-start | bytes 3145732
  2.5 0.9 %copy-start.2 = (f32[64,512]{1,0:T(8,128)S(1)}, f32[64,512]{1,0:T(8,128)}, u32[]{:S(2)}) copy-start(f32[64,512]{1,0:T(8,128)} %diffusivity_ref.1) | copy-start | bytes 393220
  3.4 0.9 %copy-start.3 = (f32[64,512]{1,0:T(8,128)S(1)}, f32[64,512]{1,0:T(8,128)}, u32[]{:S(2)}) copy-start(f32[64,512]{1,0:T(8,128)} %flow_ref.1) | copy-start | bytes 393220
  4.3 40.4 %copy-start.1 = (f32[512,512]{1,0:T(8,128)S(1)}, f32[512,512]{1,0:T(8,128)}, u32[]{:S(2)}) copy-start(f32[512,512]{1,0:T(8,128)} %modes_ref.3) | copy-start | bytes 3145732
  20.8 2.3 %copy-start.7 = (s32[256,1]{0,1:T(1,128)S(1)}, s32[256,1]{0,1:T(1,128)}, u32[]{:S(2)}) copy-start(s32[256,1]{0,1:T(1,128)} %param.12) | copy-start | bytes 3076
  20.8 2.3 %copy-start.6 = (s32[256]{0:T(256)S(1)}, s32[256]{0:T(256)}, u32[]{:S(2)}) copy-start(s32[256]{0:T(256)} %param.13) | copy-start | bytes 3076
  23.1 0.8 %copy-start.4 = (f32[128,128]{1,0:T(8,128)S(1)}, f32[128,128]{1,0:T(8,128)}, u32[]{:S(2)}) copy-start(f32[128,128]{1,0:T(8,128)} %spread_ref.1) | copy-start | bytes 196612
  23.2 0.7 %copy-start.5 = (f32[16,128]{1,0:T(8,128)S(1)}, f32[16,128]{1,0:T(8,128)}, u32[]{:S(2)}) copy-start(f32[16,128]{1,0:T(8,128)} %noise_ref.1) | copy-start | bytes 24580

commit v2 on v1

--- a/solution.py
+++ b/solution.py
@@ -165,7 +165,7 @@
     return jnp.concatenate(halves, axis=2)
 
 
-def forward_kernel(strips_ref, profile_ref, field_ref):
+def forward_step(strips_ref, profile_ref, field_ref):
     diffusion, flow = take_steps(strips_ref, 0), take_steps(strips_ref, 1)
     finest, coarse = plans(diffusion, flow, True, None)
     first = (diffusion[0] + flow[0]) * profile_ref[...]
@@ -187,7 +187,7 @@
     return jnp.where(outside, 0.0, 1.0)
 
 
-def adjoint_kernel(seg, sub, strips_ref, driving_ref, modes_ref, partial_ref):
+def adjoint_step(seg, sub, strips_ref, driving_ref, modes_ref, partial_ref):
     strip, group = lax.axis_index("seg"), lax.axis_index("sub")
     diffusion, flow = take_steps(strips_ref, 0), take_steps(strips_ref, 1)
     inside = inside_mask((1, 1, 2 * LANES), strip, seg, group, sub)
@@ -202,30 +202,16 @@
     partial_ref[...] = sums
 
 
-def enter(seg, sub, diagonal):
-    strip, group = lax.axis_index("seg"), lax.axis_index("sub")
+def enter(seg, sub):
+    count = seg * sub
+    me = lax.axis_index("seg") * sub + lax.axis_index("sub")
     barrier = pltpu.get_barrier_semaphore()
-
-    def greet(to_strip, to_group):
-        pl.semaphore_signal(barrier, inc=1, device_id=(to_strip, to_group), device_id_type=MESH)
-
-    for k in range(1, seg):
-        greet(lax.rem(strip + k, seg), group)
-    for k in range(1, sub):
-        greet(strip, lax.rem(group + k, sub))
-    if diagonal:
-
-        @pl.when(strip == 0)
-        def _():
-            for other in range(seg):
-                greet(other, lax.rem(group + sub - 1, sub))
-
-        @pl.when(strip == seg - 1)
-        def _():
-            for other in range(seg):
-                greet(other, lax.rem(group + 1, sub))
-
-    pl.semaphore_wait(barrier, seg - 1 + sub - 1 + (2 if diagonal else 0))
+    for k in range(1, count):
+        peer = lax.rem(me + k, count)
+        pl.semaphore_signal(
+            barrier, inc=1, device_id=(peer // sub, lax.rem(peer, sub)), device_id_type=MESH
+        )
+    pl.semaphore_wait(barrier, count - 1)
 
 
 def remote(source, target, send, receive, to_strip, to_group):
@@ -332,89 +318,114 @@
     return arrive, left
 
 
-def intake_kernel(seg, sub, diffusivity_ref, flow_ref, modes_ref, step_ref, strips_ref, profile_ref,
-                  packed, edges, edge_ref, steps, own, sides,
-                  seg_send, seg_recv, edge_send, edge_recv, step_send, step_recv, side_send, side_recv):
+def choose(chosen, values):
+    high = values.astype(jnp.bfloat16)
+    rest = values - high.astype(jnp.float32)
+    middle = rest.astype(jnp.bfloat16)
+    low = (rest - middle.astype(jnp.float32)).astype(jnp.bfloat16)
+    picks = chosen.astype(jnp.bfloat16)
+    parts = [jnp.dot(picks, part, preferred_element_type=jnp.float32) for part in (low, middle, high)]
+    return parts[0] + parts[1] + parts[2]
+
+
+def whole_kernel(seg, sub, diffusivity_hbm, flow_hbm, modes_hbm, step_ref, target_row_ref,
+                 target_column_ref, noise_ref, spread_ref,
+                 forward_ref, response_ref, product_ref,
+                 diffusivity, flow, modes, strips, profile, field, driving, partial_product,
+                 packed, edges, edge_in, packed_one, edges_one, edge_in_one,
+                 steps, own, sides, targets, partial, arrived, weighted, gathered, blocks, mine, products,
+                 load_sem, step_send, step_recv, side_send, side_recv, target_send, target_recv,
+                 block_send, block_recv, sum_send, sum_recv, row_send, row_recv, last_send, last_recv,
+                 seg_send, seg_recv, edge_send, edge_recv,
+                 seg_send_one, seg_recv_one, edge_send_one, edge_recv_one):
     strip, group = lax.axis_index("seg"), lax.axis_index("sub")
-    sems = (seg_send, seg_recv, edge_send, edge_recv)
-    enter(seg, sub, True)
-    arrive, left = share(
+    count = seg * sub
+    me = strip * sub + group
+    rows = diffusivity.shape[0]
+    voxel_rows = noise_ref.shape[0]
+    group_voxels = sub * voxel_rows
+
+    def place(peer):
+        return peer // sub, lax.rem(peer, sub)
+
+    def rows_of(whose):
+        return pl.ds(pl.multiple_of(whose * rows, rows), rows)
+
+    def voxels_of(whose):
+        return pl.ds(pl.multiple_of(whose * voxel_rows, voxel_rows), voxel_rows)
+
+    loads = [
+        pltpu.make_async_copy(source, target, load_sem.at[index])
+        for index, (source, target) in enumerate(
+            ((diffusivity_hbm, diffusivity), (flow_hbm, flow), (modes_hbm, modes))
+        )
+    ]
+    for load in loads:
+        load.start()
+    enter(seg, sub)
+
+    arrive_steps, left_steps = share(
         sub, group, lambda peer: step_ref, lambda whose: steps.at[whose], step_send, step_recv,
         lambda peer: (strip, peer),
     )
     steps[group] = step_ref[...]
-    copies = start_reshard(seg, sub, [diffusivity_ref[...], flow_ref[...]], packed, edges, strips_ref,
-                           edge_ref, sems)
-    arrive()
-    depth = modes_ref.shape[0] // sub
-    columns = steps[...].reshape(sub, LANES)
+    arrive_targets, left_targets = share(
+        seg, strip, lambda peer: target_row_ref.at[peer], lambda whose: targets.at[whose],
+        target_send, target_recv, lambda peer: (peer, group),
+    )
+    targets[strip] = target_row_ref[strip]
+    loads[0].wait()
+    loads[1].wait()
+    sems = (seg_send, seg_recv, edge_send, edge_recv)
+    copies = start_reshard(seg, sub, [diffusivity[...], flow[...]], packed, edges, strips, edge_in, sems)
+    loads[2].wait()
+    arrive_steps()
+    depth = modes.shape[0] // sub
+    turned = steps[...].reshape(sub, LANES).T
     total = None
-    turned = columns.T
     for whose in range(sub):
         weight = turned[:depth, whose : whose + 1]
-        term = weight * modes_ref[whose * depth : (whose + 1) * depth, :]
+        term = weight * modes[whose * depth : (whose + 1) * depth, :]
         total = term if total is None else total + term
-    profile = jnp.sum(total, axis=0, keepdims=True)
+    inlet = jnp.sum(total, axis=0, keepdims=True)
     for t in range(seg):
-        own[t + 1] = profile[:, t * LANES : (t + 1) * LANES]
+        own[t + 1] = inlet[:, t * LANES : (t + 1) * LANES]
     right = remote(own.at[seg], sides.at[0], side_send.at[0], side_recv.at[0],
                    strip, lax.rem(group + 1, sub))
     back = remote(own.at[1], sides.at[1], side_send.at[1], side_recv.at[1],
                   strip, lax.rem(group + sub - 1, sub))
     right.start()
     back.start()
-    finish_reshard(seg, sub, copies, strips_ref, edge_ref, packed, sems)
+    finish_reshard(seg, sub, copies, strips, edge_in, packed, sems)
     right.wait()
     back.wait()
     own[0] = sides[0]
     own[seg + 1] = sides[1]
     lane = lax.broadcasted_iota(jnp.int32, (1, LANES), 1)
-    profile_ref[:, :LANES] = own[strip + 1]
-    profile_ref[:, LANES:] = jnp.where(lane < HALF, own[strip + 2], own[strip])
-    left()
-
-
-def voxel_kernel(seg, sub, field_ref, target_row_ref, target_column_ref, noise_ref, spread_ref,
-                 forward_ref, response_ref, driving_ref,
-                 blocks, partial, arrived, weighted, gathered, packed, edges, edge_ref,
-                 block_send, block_recv, sum_send, sum_recv, row_send, row_recv,
-                 seg_send, seg_recv, edge_send, edge_recv):
-    strip, group = lax.axis_index("seg"), lax.axis_index("sub")
-    sems = (seg_send, seg_recv, edge_send, edge_recv)
-    rows = blocks.shape[1]
-    voxel_rows = noise_ref.shape[0]
-    enter(seg, sub, True)
-
-    def rows_of(whose):
-        return pl.ds(pl.multiple_of(whose * rows, rows), rows)
-
-    def voxels_of(whose):
-        return pl.ds(pl.multiple_of(whose * voxel_rows, voxel_rows), voxel_rows)
-
-    arrive, left_blocks = share(
-        seg, strip, lambda peer: field_ref.at[rows_of(peer), :], lambda whose: blocks.at[whose],
+    profile[:, :LANES] = own[strip + 1]
+    profile[:, LANES:] = jnp.where(lane < HALF, own[strip + 2], own[strip])
+    arrive_targets()
+
+    forward_step(strips, profile, field)
+
+    for whose in range(seg):
+        voxel = lax.broadcasted_iota(jnp.int32, (group_voxels, rows), 0)
+        chosen = jnp.where(voxel == targets[whose], 1.0, 0.0)
+        partial[whose * group_voxels : (whose + 1) * group_voxels, :] = choose(
+            chosen, field[whose * rows : (whose + 1) * rows, :]
+        )
+    arrive_sums, left_sums = share(
+        count, me, lambda peer: partial.at[voxels_of(peer), :], lambda whose: arrived.at[whose],
+        sum_send, sum_recv, place,
+    )
+    arrived[me] = partial[voxels_of(me), :]
+    arrive_blocks, left_blocks = share(
+        seg, strip, lambda peer: field.at[rows_of(peer), :], lambda whose: blocks.at[whose],
         block_send, block_recv, lambda peer: (peer, group),
     )
-    blocks[strip] = field_ref[rows_of(strip), :]
-    arrive()
-    total = None
-    for t in range(seg):
-        block = blocks[t]
-        forward_ref[:, t * LANES : (t + 1) * LANES] = block
-        voxel = lax.broadcasted_iota(jnp.int32, (sub * voxel_rows, rows), 0)
-        chosen = jnp.where(voxel == target_row_ref[t : t + 1, :], 1.0, 0.0)
-        term = jnp.dot(chosen, block, precision=HIGH, preferred_element_type=jnp.float32)
-        total = term if total is None else total + term
-    partial[...] = total
-    arrive, left_sums = share(
-        sub, group, lambda peer: partial.at[voxels_of(peer), :], lambda whose: arrived.at[whose],
-        sum_send, sum_recv, lambda peer: (strip, peer),
-    )
-    arrived[group] = partial[voxels_of(group), :]
-    arrive()
-    voxels = arrived[0]
-    for whose in range(1, sub):
-        voxels = voxels + arrived[whose]
+    blocks[strip] = field[rows_of(strip), :]
+    arrive_sums()
+    voxels = jnp.sum(arrived[...], axis=0)
     spread = spread_ref[...]
     response = lax.dot_general(
         voxels, spread, (((1,), (1,)), ((), ())), precision=HIGH, preferred_element_type=jnp.float32
@@ -423,128 +434,88 @@
     weighted[...] = jnp.dot(
         noise_ref[...] * response, spread, precision=HIGH, preferred_element_type=jnp.float32
     )
-    arrive, left_rows = share(
+    arrive_rows, left_rows = share(
         sub, group, lambda peer: weighted, lambda whose: gathered.at[voxels_of(whose), :],
         row_send, row_recv, lambda peer: (strip, peer),
     )
     gathered[voxels_of(group), :] = weighted[...]
-    arrive()
+    arrive_blocks()
+    for t in range(seg):
+        forward_ref[:, t * LANES : (t + 1) * LANES] = blocks[t]
+    arrive_rows()
     everything = gathered[...]
     tiles = []
     for t in range(seg):
-        voxel = lax.broadcasted_iota(jnp.int32, (rows, sub * voxel_rows), 1)
+        voxel = lax.broadcasted_iota(jnp.int32, (rows, group_voxels), 1)
         chosen = jnp.where(voxel == target_column_ref[:, t : t + 1], 1.0, 0.0)
-        tiles.append(jnp.dot(chosen, everything, precision=HIGH, preferred_element_type=jnp.float32))
-    copies = start_reshard(seg, sub, [jnp.concatenate(tiles, axis=1)], packed, edges, driving_ref,
-                           edge_ref, sems)
-    finish_reshard(seg, sub, copies, driving_ref, edge_ref, packed, sems)
-    left_blocks()
-    left_sums()
-    left_rows()
-
-
-def product_kernel(seg, sub, partial_ref, product_ref, mine, arrived, second, total,
-                   sub_send, sub_recv, seg_send, seg_recv):
-    strip, group = lax.axis_index("seg"), lax.axis_index("sub")
-    enter(seg, sub, False)
-    mine[...] = partial_ref[0:1, :]
-    arrive, left_first = share(
-        sub, group, lambda peer: mine, lambda whose: arrived.at[whose], sub_send, sub_recv,
-        lambda peer: (strip, peer),
-    )
-    arrived[group] = mine[...]
-    arrive()
-    value = arrived[0]
-    for whose in range(1, sub):
-        value = value + arrived[whose]
-    total[...] = value
-    arrive, left_second = share(
-        seg, strip, lambda peer: total, lambda whose: second.at[whose], seg_send, seg_recv,
-        lambda peer: (peer, group),
-    )
-    second[strip] = value
-    arrive()
-    value = second[0]
-    for whose in range(1, seg):
-        value = value + second[whose]
-    product_ref[...] = value
-    left_first()
-    left_second()
+        tiles.append(choose(chosen, everything))
+    sems = (seg_send_one, seg_recv_one, edge_send_one, edge_recv_one)
+    copies = start_reshard(seg, sub, [jnp.concatenate(tiles, axis=1)], packed_one, edges_one, driving,
+                           edge_in_one, sems)
+    finish_reshard(seg, sub, copies, driving, edge_in_one, packed_one, sems)
+
+    adjoint_step(seg, sub, strips, driving, modes, partial_product)
+
+    mine[...] = partial_product[0:1, :]
+    arrive_last, left_last = share(
+        count, me, lambda peer: mine, lambda whose: products.at[whose], last_send, last_recv, place
+    )
+    products[me] = mine[...]
+    arrive_last()
+    product_ref[...] = jnp.sum(products[...], axis=0)
+    for left in (left_steps, left_targets, left_sums, left_blocks, left_rows, left_last):
+        left()
 
 
 def on_device(seg, sub, diffusivity, background_flow, inlet_modes, profile_step, brick_owner,
               voxel_row, noise_weight, spread_matrix):
     vmem = pl.BlockSpec(memory_space=pltpu.VMEM)
+    anywhere = pl.BlockSpec(memory_space=pl.ANY)
     f32 = jnp.float32
     rows, width = diffusivity.shape
     modes = inlet_modes.shape[0]
     voxel_rows = noise_weight.shape[0]
     total_rows = rows * seg
-    dma = pltpu.SemaphoreType.DMA
-
-    def call(kernel, shapes, scratch, collective):
-        return pl.pallas_call(
-            kernel,
-            out_shape=[jax.ShapeDtypeStruct(shape, f32) for shape in shapes],
-            out_specs=[vmem] * len(shapes),
-            scratch_shapes=scratch,
-            compiler_params=pltpu.CompilerParams(
-                vmem_limit_bytes=VMEM_BYTES,
-                **({} if collective is None else {"collective_id": collective, "has_side_effects": True}),
-            ),
-        )
-
-    reshard_sems = [dma((seg,)), dma((seg,)), dma((2,)), dma((seg,))]
+    count = seg * sub
+
+    def dma(length):
+        return [pltpu.SemaphoreType.DMA((length,))] * 2
+
+    def held(*shape, dtype=f32):
+        return pltpu.VMEM(shape, dtype)
+
     step_row = jnp.pad(profile_step[None, :], ((0, 0), (0, LANES - profile_step.shape[0])))
-    strips, profile = call(
-        functools.partial(intake_kernel, seg, sub),
-        [(2, 2, total_rows, LANES), (1, 2 * LANES)],
-        [
-            pltpu.VMEM((seg, 2, 2, rows, LANES), f32),
-            pltpu.VMEM((2, 2, rows, LANES), f32),
-            pltpu.VMEM((2, total_rows, LANES), f32),
-            pltpu.VMEM((sub, 1, LANES), f32),
-            pltpu.VMEM((seg + 2, 1, LANES), f32),
-            pltpu.VMEM((2, 1, LANES), f32),
-            *reshard_sems,
-            dma((sub,)), dma((sub,)), dma((2,)), dma((2,)),
+    target = (brick_owner[:, 0] * voxel_rows + voxel_row).reshape(rows, seg)
+    forward_field, response, product = pl.pallas_call(
+        functools.partial(whole_kernel, seg, sub),
+        out_shape=[
+            jax.ShapeDtypeStruct((rows, width), f32),
+            jax.ShapeDtypeStruct((voxel_rows, LANES), f32),
+            jax.ShapeDtypeStruct((1, modes), f32),
         ],
-        0,
-    )(diffusivity, background_flow, inlet_modes, step_row)
-    (strip_field,) = call(forward_kernel, [(total_rows, LANES)], [], None)(strips, profile)
-    target = (brick_owner[:, 0] * voxel_rows + voxel_row).reshape(rows, seg)
-    forward_field, response, driving = call(
-        functools.partial(voxel_kernel, seg, sub),
-        [(rows, width), (voxel_rows, LANES), (1, 2, total_rows, LANES)],
-        [
-            pltpu.VMEM((seg, rows, LANES), f32),
-            pltpu.VMEM((sub * voxel_rows, LANES), f32),
-            pltpu.VMEM((sub, voxel_rows, LANES), f32),
-            pltpu.VMEM((voxel_rows, LANES), f32),
-            pltpu.VMEM((sub * voxel_rows, LANES), f32),
-            pltpu.VMEM((seg, 1, 2, rows, LANES), f32),
-            pltpu.VMEM((2, 1, rows, LANES), f32),
-            pltpu.VMEM((1, total_rows, LANES), f32),
-            dma((seg,)), dma((seg,)), dma((sub,)), dma((sub,)), dma((sub,)), dma((sub,)),
-            *reshard_sems,
+        in_specs=[anywhere] * 3 + [vmem] * 5,
+        out_specs=[vmem] * 3,
+        scratch_shapes=[
+            held(rows, width), held(rows, width), held(modes, width),
+            held(2, 2, total_rows, LANES), held(1, 2 * LANES), held(total_rows, LANES),
+            held(1, 2, total_rows, LANES), held(CHUNKS, modes),
+            held(seg, 2, 2, rows, LANES), held(2, 2, rows, LANES), held(2, total_rows, LANES),
+            held(seg, 1, 2, rows, LANES), held(2, 1, rows, LANES), held(1, total_rows, LANES),
+            held(sub, 1, LANES), held(seg + 2, 1, LANES), held(2, 1, LANES),
+            held(seg, 1, rows, dtype=jnp.int32),
+            held(count * voxel_rows, LANES), held(count, voxel_rows, LANES),
+            held(voxel_rows, LANES), held(sub * voxel_rows, LANES),
+            held(seg, rows, LANES), held(1, modes), held(count, 1, modes),
+            pltpu.SemaphoreType.DMA((3,)),
+            *dma(sub), *dma(2), *dma(seg), *dma(seg), *dma(count), *dma(sub), *dma(count),
+            *dma(seg), pltpu.SemaphoreType.DMA((2,)), pltpu.SemaphoreType.DMA((seg,)),
+            *dma(seg), pltpu.SemaphoreType.DMA((2,)), pltpu.SemaphoreType.DMA((seg,)),
         ],
-        1,
-    )(strip_field, target.T, target, noise_weight, spread_matrix)
-    (partial,) = call(functools.partial(adjoint_kernel, seg, sub), [(CHUNKS, modes)], [], None)(
-        strips, driving, inlet_modes
-    )
-    (product,) = call(
-        functools.partial(product_kernel, seg, sub),
-        [(1, modes)],
-        [
-            pltpu.VMEM((1, modes), f32),
-            pltpu.VMEM((sub, 1, modes), f32),
-            pltpu.VMEM((seg, 1, modes), f32),
-            pltpu.VMEM((1, modes), f32),
-            dma((sub,)), dma((sub,)), dma((seg,)), dma((seg,)),
-        ],
-        2,
-    )(partial)
+        compiler_params=pltpu.CompilerParams(
+            vmem_limit_bytes=VMEM_BYTES, collective_id=0, has_side_effects=True
+        ),
+    )(diffusivity, background_flow, inlet_modes, step_row, target.T[:, None, :], target, noise_weight,
+      spread_matrix)
     share_of = modes // (seg * sub)
     place = lax.axis_index("seg") * sub + lax.axis_index("sub")
     return (forward_field, response, lax.dynamic_slice(product[0], (place * share_of,), (share_of,)))

time: 58 us -> 55.2 us (0.952)
  Pallas kernels: 50.7 us -> 46.5 us
  other arithmetic: 0.01 us -> 1.36 us
    pallas_call x5 -> x1, Pallas kernels: 50.7 us -> 46.5 us  [on_device(): pl.pallas_call(functools.partial(whole_kernel, seg, sub), out_shape=[jax....]
    pad x1, local copies, waits for them, and re-layouts: 0.01 us -> 0.69 us  [on_device(): jnp.pad(profile_step[None, :], ((0, 0), (0, LANES - profile_step.shape[0])))]
    mul x1, other arithmetic: 0.01 us -> 0.68 us  [on_device(): target = (brick_owner[:, 0] * voxel_rows + voxel_row).reshape(rows, seg)]
    add x1, other arithmetic: 0.01 us -> 0.68 us  [on_device(): target = (brick_owner[:, 0] * voxel_rows + voxel_row).reshape(rows, seg)]
    unnamed x20 -> x12, local copies, waits for them, and re-layouts: 5.58 us -> 4.91 us
where the time goes in v2:
time: 55.2 us; the launch traced here: 54.9 us
  Pallas kernels  46.5 us (84%)
  local copies, waits for them, and re-layouts  6.36 us (12%)
  other arithmetic  1.36 us (2%)
  between operations  0.68 us (1%)
    pallas_call x1, Pallas kernels, on_device(): pl.pallas_call(functools.partial(whole_kernel, seg, sub), out_shape=[jax....  46.5 us
    unnamed x12, local copies, waits for them, and re-layouts  4.91 us

profile of v2, /device:TPU:0, one launch (start us, length us, event | category | flops | bytes accessed | tf_op | source)
XLA Modules:
  0.0 54.9 jit_solution(9048698519664215507)
XLA Ops:
  0.6 0.0 copy-start.3
  0.6 0.7 %pad.4.step_ref = f32[1,128]{1,0:T(1,128)S(1)} pad(f32[1,64]{1,0:T(1,128)} %bitcast.9, f32[]{:T(128)} %constant.7.clone.1), padding=0_0x0_64 | pad | bytes 772 | tf_op jit(solution)/shard_map/jit(_pad)/pad | solution.py:487
  1.3 0.7 %broadcast_multiply_fusion = s32[256,1]{0,1:T(1,128)S(1)} fusion(s32[256,1]{0,1:T(1,128)} %param.12), kind=kLoop, calls=%fused_computation.1 | loop fusion | flops 256 | bytes 2048 | tf_op jit(solution)/shard_map/mul | solution.py:488
  2.0 0.7 %add.11 = s32[256]{0:T(256)S(1)} add(s32[256]{0:T(256)S(1)} %bitcast.8, s32[256]{0:T(256)} %param.13) | non-fusion elementwise | flops 256 | bytes 3072 | tf_op jit(solution)/shard_map/add | solution.py:488
  2.7 0.1 reshape.12.target_column_ref
  2.8 0.0 copy-start.4
  2.8 0.1 copy.12
  2.9 0.0 copy-done.3
  2.9 0.6 %copy-done.4 = f32[16,128]{1,0:T(8,128)S(1)} copy-done((f32[16,128]{1,0:T(8,128)S(1)}, f32[16,128]{1,0:T(8,128)}, u32[]{:S(2)}) %copy-start.4) | copy-done | bytes 8216
  3.5 0.0 copy-start
  3.5 1.2 %copy-done = f32[512,512]{1,0:T(8,128)S(1)} copy-done((f32[512,512]{1,0:T(8,128)S(1)}, f32[512,512]{1,0:T(8,128)}, u32[]{:S(2)}) %copy-start) | copy-done | bytes 1048600
  4.7 0.0 copy-start.1
  4.7 0.9 %copy-done.1 = f32[64,512]{1,0:T(8,128)S(1)} copy-done((f32[64,512]{1,0:T(8,128)S(1)}, f32[64,512]{1,0:T(8,128)}, u32[]{:S(2)}) %copy-start.1) | copy-done | bytes 131096
  5.6 0.0 copy-start.2
  5.6 0.9 %copy-done.2 = f32[64,512]{1,0:T(8,128)S(1)} copy-done((f32[64,512]{1,0:T(8,128)S(1)}, f32[64,512]{1,0:T(8,128)}, u32[]{:S(2)}) %copy-start.2) | copy-done | bytes 131096
  6.5 46.5 %shard_map.103 = (f32[64,512]{1,0:T(8,128)S(1)}, f32[16,128]{1,0:T(8,128)S(1)}, f32[1,512]{1,0:T(1,128)S(1)}) custom-call(f32[64,512]{1,0:T(8,128)S(1)} %copy-done.1, f32[64,512]{1,0:T(8,128)S(1)} %copy-done.2, f32[512,512]{1,0:T(8,128)S(1)} %copy-done, f32[1,128]{1,0:T(1,128)S(1)} %pad.4.step_ref, s32[4,1,64]{2,1,0:T(1,128)S(1)} %bitcast.7, ...), custom_call_target="tpu_custom_call" | custom-call | tf_op jit(solution)/shard_map/pallas_call | solution.py:489
  53.1 0.6 %dynamic-slice_bitcast_fusion = f32[16]{0:T(128)} fusion(f32[1,512]{1,0:T(1,128)S(1)} %get-tuple-element.8, s32[]{:T(128)S(6)} %select_n.3), kind=kLoop, calls=%fused_computation | loop fusion | bytes 132 | tf_op jit(solution)/shard_map/dynamic_slice | solution.py:521
  53.7 0.7 %copy.15 = f32[64,512]{1,0:T(8,128)} copy(f32[64,512]{1,0:T(8,128)S(1)} %get-tuple-element.12) | data formatting | bytes 262144
  54.3 0.6 %copy.16 = f32[16,128]{1,0:T(8,128)} copy(f32[16,128]{1,0:T(8,128)S(1)} %get-tuple-element.13) | data formatting | bytes 16384
Async XLA Ops:
  0.6 2.3 %copy-start.3 = (f32[128,128]{1,0:T(8,128)S(1)}, f32[128,128]{1,0:T(8,128)}, u32[]{:S(2)}) copy-start(f32[128,128]{1,0:T(8,128)} %spread_ref.1) | copy-start | bytes 196612
  2.8 0.7 %copy-start.4 = (f32[16,128]{1,0:T(8,128)S(1)}, f32[16,128]{1,0:T(8,128)}, u32[]{:S(2)}) copy-start(f32[16,128]{1,0:T(8,128)} %noise_ref.1) | copy-start | bytes 24580
  3.5 1.2 %copy-start = (f32[512,512]{1,0:T(8,128)S(1)}, f32[512,512]{1,0:T(8,128)}, u32[]{:S(2)}) copy-start(f32[512,512]{1,0:T(8,128)} %modes_hbm.1) | copy-start | bytes 3145732
  4.7 0.9 %copy-start.1 = (f32[64,512]{1,0:T(8,128)S(1)}, f32[64,512]{1,0:T(8,128)}, u32[]{:S(2)}) copy-start(f32[64,512]{1,0:T(8,128)} %diffusivity_hbm.1) | copy-start | bytes 393220
  5.6 0.9 %copy-start.2 = (f32[64,512]{1,0:T(8,128)S(1)}, f32[64,512]{1,0:T(8,128)}, u32[]{:S(2)}) copy-start(f32[64,512]{1,0:T(8,128)} %flow_hbm.1) | copy-start | bytes 393220

commit v3 on v2

--- a/solution.py
+++ b/solution.py
@@ -15,7 +15,7 @@
 LANES = 128
 HALF = LANES // 2
 CHUNKS = 8
-VMEM_BYTES = 48 * 1024 * 1024
+VMEM_BYTES = 60 * 1024 * 1024
 
 
 def lane_shift(value, amount):
@@ -203,15 +203,28 @@
 
 
 def enter(seg, sub):
-    count = seg * sub
-    me = lax.axis_index("seg") * sub + lax.axis_index("sub")
+    strip, group = lax.axis_index("seg"), lax.axis_index("sub")
     barrier = pltpu.get_barrier_semaphore()
-    for k in range(1, count):
-        peer = lax.rem(me + k, count)
-        pl.semaphore_signal(
-            barrier, inc=1, device_id=(peer // sub, lax.rem(peer, sub)), device_id_type=MESH
-        )
-    pl.semaphore_wait(barrier, count - 1)
+
+    def greet(to_strip, to_group):
+        pl.semaphore_signal(barrier, inc=1, device_id=(to_strip, to_group), device_id_type=MESH)
+
+    for k in range(1, seg):
+        greet(lax.rem(strip + k, seg), group)
+    for k in range(1, sub):
+        greet(strip, lax.rem(group + k, sub))
+
+    @pl.when(strip == 0)
+    def _():
+        for other in range(seg):
+            greet(other, lax.rem(group + sub - 1, sub))
+
+    @pl.when(strip == seg - 1)
+    def _():
+        for other in range(seg):
+            greet(other, lax.rem(group + 1, sub))
+
+    pl.semaphore_wait(barrier, seg - 1 + sub - 1 + 2)
 
 
 def remote(source, target, send, receive, to_strip, to_group):
@@ -225,76 +238,94 @@
     )
 
 
-def start_reshard(seg, sub, fields, packed, edges, strips_ref, edge_ref, sems):
+def join_halos(one, other):
+    lane = lax.broadcasted_iota(jnp.int32, one.shape, 1)
+    quarter = HALF // 2
+    inner = jnp.where(lane < HALF, lane_shift(other, quarter), lane_shift(other, -quarter))
+    return jnp.where((lane < quarter) | (lane >= LANES - quarter), one, inner)
+
+
+def split_halos(joined):
+    lane = lax.broadcasted_iota(jnp.int32, joined.shape, 1)
+    quarter = HALF // 2
+    other = jnp.where(lane < HALF, lane_shift(joined, -quarter), lane_shift(joined, quarter))
+    return joined, other
+
+
+def join_fields(fields):
+    if len(fields) == 2:
+        return join_halos(*fields)
+    middle = fields[0].shape[0] // 2
+    return join_halos(fields[0][:middle], fields[0][middle:])
+
+
+def start_reshard(seg, sub, fields, packed, edges, inbox, edge_in, sems):
     seg_send, seg_recv, edge_send, edge_recv = sems
     strip, group = lax.axis_index("seg"), lax.axis_index("sub")
-    rows = packed.shape[3]
+    rows = fields[0].shape[0]
+    tiles = [[field[:, t * LANES : (t + 1) * LANES] for t in range(seg)] for field in fields]
     lane = lax.broadcasted_iota(jnp.int32, (rows, LANES), 1)
-    for index, field in enumerate(fields):
-        edges[0, index] = field[:, (seg - 1) * LANES : seg * LANES]
-        edges[1, index] = field[:, :LANES]
-    here = pl.ds(pl.multiple_of(strip * rows, rows), rows)
-    copies = [
-        remote(edges.at[0], edge_ref.at[:, here, :], edge_send.at[0], edge_recv.at[strip],
-               0, lax.rem(group + 1, sub)),
-        remote(edges.at[1], edge_ref.at[:, here, :], edge_send.at[1], edge_recv.at[strip],
-               seg - 1, lax.rem(group + sub - 1, sub)),
-    ]
-    for copy in copies:
-        copy.start()
-    for index, field in enumerate(fields):
-        tiles = [field[:, t * LANES : (t + 1) * LANES] for t in range(seg)]
-        for t in range(seg):
-            packed[t, index, 0] = tiles[t]
-            packed[t, index, 1] = jnp.where(
-                lane < HALF, tiles[min(t + 1, seg - 1)], tiles[max(t - 1, 0)]
-            )
+    mains = len(fields) * rows
+    for t in range(seg):
+        halos = []
+        for index, row in enumerate(tiles):
+            packed[t, index * rows : (index + 1) * rows, :] = row[t]
+            halos.append(jnp.where(lane < HALF, row[min(t + 1, seg - 1)], row[max(t - 1, 0)]))
+        packed[t, mains:, :] = join_fields(halos)
+    copies = []
     for k in range(1, seg):
         peer = lax.rem(strip + k, seg)
-        copy = remote(packed.at[peer], strips_ref.at[:, :, here, :], seg_send.at[k], seg_recv.at[strip],
-                      peer, group)
-        copy.start()
-        copies.append(copy)
-    strips_ref[:, :, here, :] = packed[strip]
+        copies.append(remote(packed.at[peer], inbox.at[strip], seg_send.at[k], seg_recv.at[strip],
+                             peer, group))
+        copies[-1].start()
+    edges[0] = join_fields([row[seg - 1] for row in tiles])
+    edges[1] = join_fields([row[0] for row in tiles])
+    for side, (to_strip, to_group) in enumerate(((0, group + 1), (seg - 1, group + sub - 1))):
+        copies.append(remote(edges.at[side], edge_in.at[strip], edge_send.at[side], edge_recv.at[strip],
+                             to_strip, lax.rem(to_group, sub)))
+        copies[-1].start()
+    inbox[strip] = packed[strip]
     return copies
 
 
-def finish_reshard(seg, sub, copies, strips_ref, edge_ref, packed, sems):
+def finish_reshard(seg, sub, copies, strips, packed, edges, inbox, edge_in, sems):
     seg_send, seg_recv, edge_send, edge_recv = sems
     strip, group = lax.axis_index("seg"), lax.axis_index("sub")
-    rows = packed.shape[3]
+    fields, rows = strips.shape[0], strips.shape[2] // seg
+    mains = fields * rows
     for k in range(1, seg):
         peer = lax.rem(strip + k, seg)
-        there = pl.ds(pl.multiple_of(peer * rows, rows), rows)
-        remote(packed.at[peer], strips_ref.at[:, :, there, :], seg_send.at[k], seg_recv.at[peer],
-               peer, group).wait_recv()
-
-    def edge_arrivals():
+        remote(packed.at[peer], inbox.at[peer], seg_send.at[k], seg_recv.at[peer], peer,
+               group).wait_recv()
+
+    def take_edges(known, outer):
         for other in range(seg):
-            there = pl.ds(other * rows, rows)
-            remote(packed.at[other, :, 0], edge_ref.at[:, there, :], edge_send.at[0],
-                   edge_recv.at[other], 0, group).wait_recv()
-
-    lane = lax.broadcasted_iota(jnp.int32, edge_ref.shape, 2)
+            remote(edges.at[0], edge_in.at[other], edge_send.at[0], edge_recv.at[other], 0,
+                   group).wait_recv()
+            kept = inbox[other, mains:, :]
+            lane = lax.broadcasted_iota(jnp.int32, kept.shape, 1)
+            use = lane >= HALF if outer else lane < HALF
+            inbox[other, mains:, :] = jnp.where(use, edge_in[other] * known, kept)
 
     @pl.when(strip == 0)
     def _():
-        edge_arrivals()
-        known = jnp.where(group > 0, 1.0, 0.0)
-        strips_ref[:, 1] = jnp.where(
-            lane >= HALF, edge_ref[...] * known, strips_ref[:, 1]
-        )
+        take_edges(jnp.where(group > 0, 1.0, 0.0), True)
 
     @pl.when(strip == seg - 1)
     def _():
-        edge_arrivals()
-        known = jnp.where(group < sub - 1, 1.0, 0.0)
-        strips_ref[:, 1] = jnp.where(
-            lane < HALF, edge_ref[...] * known, strips_ref[:, 1]
-        )
-
-    for copy in copies:
-        copy.wait_send()
+        take_edges(jnp.where(group < sub - 1, 1.0, 0.0), False)
+
+    for other in range(seg):
+        start = other * rows
+        halos = split_halos(inbox[other, mains:, :])
+        for index in range(fields):
+            strips[index, 0, start : start + rows, :] = inbox[other, index * rows : (index + 1) * rows, :]
+        if fields == 2:
+            strips[0, 1, start : start + rows, :] = halos[0]
+            strips[1, 1, start : start + rows, :] = halos[1]
+        else:
+            strips[0, 1, start : start + rows // 2, :] = halos[0]
+            strips[0, 1, start + rows // 2 : start + rows, :] = halos[1]
 
 
 def share(count, me, source_of, target_of, send, recv, place):
@@ -328,25 +359,22 @@
     return parts[0] + parts[1] + parts[2]
 
 
-def whole_kernel(seg, sub, diffusivity_hbm, flow_hbm, modes_hbm, step_ref, target_row_ref,
-                 target_column_ref, noise_ref, spread_ref,
+def whole_kernel(seg, sub, diffusivity_hbm, flow_hbm, modes_hbm, step_ref, owner_ref, voxel_row_ref,
+                 noise_ref, spread_ref,
                  forward_ref, response_ref, product_ref,
                  diffusivity, flow, modes, strips, profile, field, driving, partial_product,
-                 packed, edges, edge_in, packed_one, edges_one, edge_in_one,
-                 steps, own, sides, targets, partial, arrived, weighted, gathered, blocks, mine, products,
-                 load_sem, step_send, step_recv, side_send, side_recv, target_send, target_recv,
-                 block_send, block_recv, sum_send, sum_recv, row_send, row_recv, last_send, last_recv,
+                 packed, edges, inbox, edge_in, packed_one, edges_one, inbox_one, edge_in_one,
+                 step_row, steps, own, sides, targets, selected,
+                 partial, arrived, weighted, gathered, blocks, mine, products, total_row, second,
+                 load_sem, step_send, step_recv, side_send, side_recv,
+                 block_send, block_recv, sum_send, sum_recv, row_send, row_recv,
+                 first_send, first_recv, second_send, second_recv,
                  seg_send, seg_recv, edge_send, edge_recv,
                  seg_send_one, seg_recv_one, edge_send_one, edge_recv_one):
     strip, group = lax.axis_index("seg"), lax.axis_index("sub")
-    count = seg * sub
-    me = strip * sub + group
     rows = diffusivity.shape[0]
     voxel_rows = noise_ref.shape[0]
     group_voxels = sub * voxel_rows
-
-    def place(peer):
-        return peer // sub, lax.rem(peer, sub)
 
     def rows_of(whose):
         return pl.ds(pl.multiple_of(whose * rows, rows), rows)
@@ -362,22 +390,23 @@
     ]
     for load in loads:
         load.start()
+    target = owner_ref[...] * voxel_rows + voxel_row_ref[...]
+    for part in range(target.shape[0]):
+        spread_out = jnp.broadcast_to(target[part : part + 1, :], (LANES, LANES))
+        targets[part * LANES : (part + 1) * LANES, :] = spread_out.T
+    step_row[...] = jnp.zeros_like(step_row)
+    step_row[:, : step_ref.shape[1]] = step_ref[...]
     enter(seg, sub)
 
     arrive_steps, left_steps = share(
-        sub, group, lambda peer: step_ref, lambda whose: steps.at[whose], step_send, step_recv,
+        sub, group, lambda peer: step_row, lambda whose: steps.at[whose], step_send, step_recv,
         lambda peer: (strip, peer),
     )
-    steps[group] = step_ref[...]
-    arrive_targets, left_targets = share(
-        seg, strip, lambda peer: target_row_ref.at[peer], lambda whose: targets.at[whose],
-        target_send, target_recv, lambda peer: (peer, group),
-    )
-    targets[strip] = target_row_ref[strip]
+    steps[group] = step_row[...]
     loads[0].wait()
     loads[1].wait()
     sems = (seg_send, seg_recv, edge_send, edge_recv)
-    copies = start_reshard(seg, sub, [diffusivity[...], flow[...]], packed, edges, strips, edge_in, sems)
+    copies = start_reshard(seg, sub, [diffusivity[...], flow[...]], packed, edges, inbox, edge_in, sems)
     loads[2].wait()
     arrive_steps()
     depth = modes.shape[0] // sub
@@ -396,35 +425,44 @@
                   strip, lax.rem(group + sub - 1, sub))
     right.start()
     back.start()
-    finish_reshard(seg, sub, copies, strips, edge_in, packed, sems)
-    right.wait()
-    back.wait()
+    finish_reshard(seg, sub, copies, strips, packed, edges, inbox, edge_in, sems)
+    right.wait_recv()
+    back.wait_recv()
+    sent = copies + [right, back]
     own[0] = sides[0]
     own[seg + 1] = sides[1]
     lane = lax.broadcasted_iota(jnp.int32, (1, LANES), 1)
     profile[:, :LANES] = own[strip + 1]
     profile[:, LANES:] = jnp.where(lane < HALF, own[strip + 2], own[strip])
-    arrive_targets()
 
     forward_step(strips, profile, field)
 
-    for whose in range(seg):
-        voxel = lax.broadcasted_iota(jnp.int32, (group_voxels, rows), 0)
-        chosen = jnp.where(voxel == targets[whose], 1.0, 0.0)
-        partial[whose * group_voxels : (whose + 1) * group_voxels, :] = choose(
-            chosen, field[whose * rows : (whose + 1) * rows, :]
-        )
-    arrive_sums, left_sums = share(
-        count, me, lambda peer: partial.at[voxels_of(peer), :], lambda whose: arrived.at[whose],
-        sum_send, sum_recv, place,
-    )
-    arrived[me] = partial[voxels_of(me), :]
-    arrive_blocks, left_blocks = share(
+    arrive, left_blocks = share(
         seg, strip, lambda peer: field.at[rows_of(peer), :], lambda whose: blocks.at[whose],
         block_send, block_recv, lambda peer: (peer, group),
     )
     blocks[strip] = field[rows_of(strip), :]
-    arrive_sums()
+    voxel = lax.broadcasted_iota(jnp.int32, (rows, LANES), 1)
+    picks = []
+    for t in range(seg):
+        wanted = targets[pl.ds(t, rows, stride=seg), :]
+        picks.append(jnp.concatenate(
+            [jnp.where(voxel + start == wanted, 1.0, 0.0) for start in range(0, group_voxels, LANES)],
+            axis=1,
+        ))
+    picks_by_voxel = [pick.T for pick in picks]
+    arrive()
+    partial[...] = choose(
+        jnp.concatenate(picks_by_voxel, axis=1), jnp.concatenate([blocks[t] for t in range(seg)], axis=0)
+    )
+    arrive, left_sums = share(
+        sub, group, lambda peer: partial.at[voxels_of(peer), :], lambda whose: arrived.at[whose],
+        sum_send, sum_recv, lambda peer: (strip, peer),
+    )
+    arrived[group] = partial[voxels_of(group), :]
+    for t in range(seg):
+        forward_ref[:, t * LANES : (t + 1) * LANES] = blocks[t]
+    arrive()
     voxels = jnp.sum(arrived[...], axis=0)
     spread = spread_ref[...]
     response = lax.dot_general(
@@ -439,44 +477,46 @@
         row_send, row_recv, lambda peer: (strip, peer),
     )
     gathered[voxels_of(group), :] = weighted[...]
-    arrive_blocks()
-    for t in range(seg):
-        forward_ref[:, t * LANES : (t + 1) * LANES] = blocks[t]
     arrive_rows()
-    everything = gathered[...]
-    tiles = []
-    for t in range(seg):
-        voxel = lax.broadcasted_iota(jnp.int32, (rows, group_voxels), 1)
-        chosen = jnp.where(voxel == target_column_ref[:, t : t + 1], 1.0, 0.0)
-        tiles.append(choose(chosen, everything))
+    selected[...] = choose(jnp.concatenate(picks, axis=0), gathered[...])
+    tiles = [selected[t * rows : (t + 1) * rows, :] for t in range(seg)]
     sems = (seg_send_one, seg_recv_one, edge_send_one, edge_recv_one)
-    copies = start_reshard(seg, sub, [jnp.concatenate(tiles, axis=1)], packed_one, edges_one, driving,
+    copies = start_reshard(seg, sub, [jnp.concatenate(tiles, axis=1)], packed_one, edges_one, inbox_one,
                            edge_in_one, sems)
-    finish_reshard(seg, sub, copies, driving, edge_in_one, packed_one, sems)
+    finish_reshard(seg, sub, copies, driving, packed_one, edges_one, inbox_one, edge_in_one, sems)
 
     adjoint_step(seg, sub, strips, driving, modes, partial_product)
 
     mine[...] = partial_product[0:1, :]
-    arrive_last, left_last = share(
-        count, me, lambda peer: mine, lambda whose: products.at[whose], last_send, last_recv, place
-    )
-    products[me] = mine[...]
-    arrive_last()
-    product_ref[...] = jnp.sum(products[...], axis=0)
-    for left in (left_steps, left_targets, left_sums, left_blocks, left_rows, left_last):
+    arrive, left_first = share(
+        sub, group, lambda peer: mine, lambda whose: products.at[whose], first_send, first_recv,
+        lambda peer: (strip, peer),
+    )
+    products[group] = mine[...]
+    arrive()
+    total_row[...] = jnp.sum(products[...], axis=0)
+    arrive, left_second = share(
+        seg, strip, lambda peer: total_row, lambda whose: second.at[whose], second_send, second_recv,
+        lambda peer: (peer, group),
+    )
+    second[strip] = total_row[...]
+    arrive()
+    product_ref[...] = jnp.sum(second[...], axis=0)
+    for left in (left_steps, left_blocks, left_sums, left_rows, left_first, left_second):
         left()
+    for copy in sent + copies:
+        copy.wait_send()
 
 
 def on_device(seg, sub, diffusivity, background_flow, inlet_modes, profile_step, brick_owner,
               voxel_row, noise_weight, spread_matrix):
     vmem = pl.BlockSpec(memory_space=pltpu.VMEM)
-    anywhere = pl.BlockSpec(memory_space=pl.ANY)
+    anywhere = pl.BlockSpec(memory_space=pltpu.HBM)
     f32 = jnp.float32
     rows, width = diffusivity.shape
     modes = inlet_modes.shape[0]
     voxel_rows = noise_weight.shape[0]
     total_rows = rows * seg
-    count = seg * sub
 
     def dma(length):
         return [pltpu.SemaphoreType.DMA((length,))] * 2
@@ -484,8 +524,7 @@
     def held(*shape, dtype=f32):
         return pltpu.VMEM(shape, dtype)
 
-    step_row = jnp.pad(profile_step[None, :], ((0, 0), (0, LANES - profile_step.shape[0])))
-    target = (brick_owner[:, 0] * voxel_rows + voxel_row).reshape(rows, seg)
+    blocks = brick_owner.shape[0]
     forward_field, response, product = pl.pallas_call(
         functools.partial(whole_kernel, seg, sub),
         out_shape=[
@@ -499,23 +538,26 @@
             held(rows, width), held(rows, width), held(modes, width),
             held(2, 2, total_rows, LANES), held(1, 2 * LANES), held(total_rows, LANES),
             held(1, 2, total_rows, LANES), held(CHUNKS, modes),
-            held(seg, 2, 2, rows, LANES), held(2, 2, rows, LANES), held(2, total_rows, LANES),
-            held(seg, 1, 2, rows, LANES), held(2, 1, rows, LANES), held(1, total_rows, LANES),
-            held(sub, 1, LANES), held(seg + 2, 1, LANES), held(2, 1, LANES),
-            held(seg, 1, rows, dtype=jnp.int32),
-            held(count * voxel_rows, LANES), held(count, voxel_rows, LANES),
+            held(seg, 3 * rows, LANES), held(2, rows, LANES),
+            held(seg, 3 * rows, LANES), held(seg, rows, LANES),
+            held(seg, 3 * rows // 2, LANES), held(2, rows // 2, LANES),
+            held(seg, 3 * rows // 2, LANES), held(seg, rows // 2, LANES),
+            held(1, LANES), held(sub, 1, LANES), held(seg + 2, 1, LANES), held(2, 1, LANES),
+            held(blocks, LANES, dtype=jnp.int32), held(blocks, LANES),
+            held(sub * voxel_rows, LANES), held(sub, voxel_rows, LANES),
             held(voxel_rows, LANES), held(sub * voxel_rows, LANES),
-            held(seg, rows, LANES), held(1, modes), held(count, 1, modes),
+            held(seg, rows, LANES), held(1, modes), held(sub, 1, modes), held(1, modes),
+            held(seg, 1, modes),
             pltpu.SemaphoreType.DMA((3,)),
-            *dma(sub), *dma(2), *dma(seg), *dma(seg), *dma(count), *dma(sub), *dma(count),
+            *dma(sub), *dma(2), *dma(seg), *dma(sub), *dma(sub), *dma(sub), *dma(seg),
             *dma(seg), pltpu.SemaphoreType.DMA((2,)), pltpu.SemaphoreType.DMA((seg,)),
             *dma(seg), pltpu.SemaphoreType.DMA((2,)), pltpu.SemaphoreType.DMA((seg,)),
         ],
         compiler_params=pltpu.CompilerParams(
             vmem_limit_bytes=VMEM_BYTES, collective_id=0, has_side_effects=True
         ),
-    )(diffusivity, background_flow, inlet_modes, step_row, target.T[:, None, :], target, noise_weight,
-      spread_matrix)
+    )(diffusivity, background_flow, inlet_modes, profile_step.reshape(1, -1),
+      brick_owner.reshape(-1, LANES), voxel_row.reshape(-1, LANES), noise_weight, spread_matrix)
     share_of = modes // (seg * sub)
     place = lax.axis_index("seg") * sub + lax.axis_index("sub")
     return (forward_field, response, lax.dynamic_slice(product[0], (place * share_of,), (share_of,)))

time: 55.2 us -> 48.9 us (0.89)
  local copies, waits for them, and re-layouts: 6.36 us -> 3.39 us
  Pallas kernels: 46.5 us -> 44.6 us
  other arithmetic: 1.36 us -> 0 us
    unnamed x12 -> x4, local copies, waits for them, and re-layouts: 4.91 us -> 2.18 us
    pallas_call x1, Pallas kernels: 46.5 us -> 44.6 us  [on_device(): pl.pallas_call(functools.partial(whole_kernel, seg, sub), out_shape=[jax....]
    pad x1 -> x0, local copies, waits for them, and re-layouts: 0.69 us -> none  [on_device(): jnp.pad(profile_step[None, :], ((0, 0), (0, LANES - profile_step.shape[0])))]
    add x1 -> x0, other arithmetic: 0.68 us -> none  [on_device(): target = (brick_owner[:, 0] * voxel_rows + voxel_row).reshape(rows, seg)]
    mul x1 -> x0, other arithmetic: 0.68 us -> none  [on_device(): target = (brick_owner[:, 0] * voxel_rows + voxel_row).reshape(rows, seg)]
    dynamic_slice x1, local copies, waits for them, and re-layouts: 0.59 us -> 1.21 us  [on_device(): lax.dynamic_slice(product[0], (place * share_of,), (share_of,))]
where the time goes in v3:
time: 48.9 us; the launch traced here: 48.7 us
  Pallas kernels  44.6 us (91%)
  local copies, waits for them, and re-layouts  3.39 us (7%)
  between operations  0.65 us (1%)
    pallas_call x1, Pallas kernels, on_device(): pl.pallas_call(functools.partial(whole_kernel, seg, sub), out_shape=[jax....  44.6 us
    unnamed x4, local copies, waits for them, and re-layouts  2.18 us
    dynamic_slice x1, local copies, waits for them, and re-layouts, on_device(): lax.dynamic_slice(product[0], (place * share_of,), (share_of,))  1.21 us

profile of v3, /device:TPU:0, one launch (start us, length us, event | category | flops | bytes accessed | tf_op | source)
XLA Modules:
  0.0 48.7 jit_solution(15266011376910868964)
XLA Ops:
  0.6 44.6 %shard_map.103 = (f32[64,512]{1,0:T(8,128)}, f32[16,128]{1,0:T(8,128)}, f32[1,512]{1,0:T(1,128)}) custom-call(f32[64,512]{1,0:T(8,128)} %diffusivity_hbm.1, f32[64,512]{1,0:T(8,128)} %flow_hbm.1, f32[512,512]{1,0:T(8,128)} %modes_hbm.1, f32[1,64]{1,0:T(1,128)} %bitcast.7, s32[2,128]{1,0:T(2,128)} %bitcast.5, s32[2,128]{1,0:T(2,128)} %bitcast.6, ...), custom_call_target="tpu_custom_call" | custom-call | tf_op jit(solution)/shard_map/pallas_call | solution.py:528
  45.3 1.2 %dynamic-slice_bitcast_fusion = f32[16]{0:T(128)} fusion(f32[1,512]{1,0:T(1,128)} %get-tuple-element.8, s32[]{:T(128)S(6)} %select_n.3), kind=kLoop, calls=%fused_computation | loop fusion | bytes 132 | tf_op jit(solution)/shard_map/dynamic_slice | solution.py:563
  46.5 0.0 copy-start
  46.5 1.6 %copy.13 = f32[64,512]{1,0:T(8,128)} copy(f32[64,512]{1,0:T(8,128)} %get-tuple-element.12) | data formatting | bytes 262144
  48.1 0.0 copy-done
  48.1 0.6 %copy.14 = f32[16,128]{1,0:T(8,128)} copy(f32[16,128]{1,0:T(8,128)S(1)} %copy-done) | data formatting | bytes 16384
Async XLA Ops:
  46.5 1.6 %copy-start = (f32[16,128]{1,0:T(8,128)S(1)}, f32[16,128]{1,0:T(8,128)}, u32[]{:S(2)}) copy-start(f32[16,128]{1,0:T(8,128)} %get-tuple-element.13) | copy-start | bytes 24580
